TPU v7x, 256 devices: a whole 4x4x8 slice. The times are simulated.
256 devices in a mesh: tok: 4 (over z_lo, core), voc: 64 (over z_hi, y, x).
Axes of the slice: x: 4, y: 4, z: 8 (z_hi: 4, z_lo: 2; z = z_hi * 2 + z_lo), core: 2. Of those that a mesh axis runs over, the one named last changes fastest.
Arguments:
- hidden_states: bfloat16 [1024, 3584], P('tok'), may hold values from -12 to 12
- student_head: bfloat16 [3584, 131072], P('tok', 'voc'), may hold values from -0.5 to 0.5
- teacher_logits: bfloat16 [1024, 131072], P(('tok', 'voc')), may hold values from -16 to 320
- quality: float32 [1024], P('tok'), may hold values from 0.25 to 4
Outputs:
- hidden_grad: bfloat16 [1024, 3584], P('tok', 'voc')
- head_grad: bfloat16 [3584, 131072], P('tok', 'voc')
All inputs are finite; a program needn't handle non-finite values.
Results may differ from a plain program's by a relative error of at most 0.0121.
Values may be sent and summed in bfloat16 or wider, within the bound.
A program may use at most 128 MiB of HBM per device.

v0:
```python
import jax
import jax.numpy as jnp
from jax import lax
from jax.sharding import PartitionSpec as P

loss_scale = 64.0


def body(hidden_states, student_head, teacher_logits, quality):
    head_full = lax.all_gather(student_head, "tok", axis=0, tiled=True)
    arrived = lax.all_to_all(teacher_logits, "voc", split_axis=1, concat_axis=0, tiled=True)
    student = jnp.dot(hidden_states, head_full, preferred_element_type=jnp.float32)
    teacher = arrived.astype(jnp.float32)
    teacher_top = lax.pmax(jnp.max(teacher, axis=1, keepdims=True), "voc")
    teacher_sum = lax.psum(jnp.sum(jnp.exp(teacher - teacher_top), axis=1, keepdims=True), "voc")
    teacher_lse = teacher_top + jnp.log(teacher_sum)
    local_top = jnp.max(student, axis=1, keepdims=True)
    student_top = lax.pmax(local_top, "voc")
    student_sum = lax.psum(jnp.sum(jnp.exp(student - student_top), axis=1, keepdims=True), "voc")
    student_lse = student_top + jnp.log(student_sum)
    diff = jnp.exp(student - student_lse) - jnp.exp(teacher - teacher_lse)
    grads = (loss_scale * quality[:, None] * diff).astype(jnp.bfloat16)
    partial_hidden = lax.dot_general(
        grads, head_full, (((1,), (1,)), ((), ())), preferred_element_type=jnp.float32
    )
    hidden_grad = lax.psum_scatter(partial_hidden, "voc", scatter_dimension=1, tiled=True).astype(
        jnp.bfloat16
    )
    head_total = lax.psum_scatter(
        lax.dot_general(
            hidden_states, grads, (((0,), (0,)), ((), ())), preferred_element_type=jnp.float32
        ).astype(jnp.bfloat16),
        "tok",
        scatter_dimension=0,
        tiled=True,
    )
    return (hidden_grad, head_total)


def solution(mesh):
    return jax.shard_map(
        body,
        mesh=mesh,
        in_specs=(P("tok", None), P("tok", "voc"), P(("tok", "voc"), None), P("tok")),
        out_specs=(P("tok", "voc"), P("tok", "voc")),
        check_vma=False,
    )
```

profile of v0, /device:TPU:1, one launch (start us, length us, event | category | flops | bytes accessed | tf_op | source)
XLA Modules:
  0.0 1090.6 jit_solution(11755068139850644695)
XLA Ops:
  7.2 0.0 copy-start
  7.2 0.0 copy-start.1
  7.2 0.0 all-gather.2.cloned.1.call-start
  7.2 0.7 all-gather.2.cloned.1.call-update
  7.9 15.1 %all-to-all-start = ((bf16[4,64,2048]{2,0,1:T(4,128)(2,1)}), bf16[4,64,2048]{2,0,1:T(4,128)(2,1)S(1)}, u32[]{:S(2)}, u32[]{:S(2)}) async-start(bf16[4,64,2048]{2,0,1:T(4,128)(2,1)} %bitcast.21), calls=%async_computation | async-start | bytes 2097152 | tf_op jit(solution)/shard_map/all_to_all | solution.py:11
  23.1 0.0 reduce-scatter.5.cloned.1.call-start
  23.1 0.0 copy-done.1
  23.1 33.6 %all-to-all-done = bf16[4,64,2048]{2,0,1:T(4,128)(2,1)S(1)} async-done(((bf16[4,64,2048]{2,0,1:T(4,128)(2,1)}), bf16[4,64,2048]{2,0,1:T(4,128)(2,1)S(1)}, u32[]{:S(2)}, u32[]{:S(2)}) %all-to-all-start) | async-done | bytes 1048608 | tf_op jit(solution)/shard_map/all_to_all | solution.py:11
  56.8 0.5 bitcast_reduce_fusion
  57.3 0.1 reshape.33
  57.4 1.5 bitcast_convert_fusion
  58.9 3.0 reshape.32
  61.9 103.4 %all-gather.2.cloned.1.call-done = bf16[3584,2048]{1,0:T(8,128)(2,1)} async-done(((bf16[896,2048]{1,0:T(8,128)(2,1)}), bf16[3584,2048]{1,0:T(8,128)(2,1)}) %all-gather.2.cloned.1.call-update) | async-done | bytes 14680080 | tf_op jit(solution)/shard_map/all_gather | solution.py:10
  165.3 0.0 copy-done
  165.3 8.9 fusion.1
  174.2 165.5 %all-reduce.1 = (f32[256,1]{0,1:T(1,128)S(1)}, f32[256,1]{0,1:T(1,128)S(1)}) all-reduce(f32[256,1]{0,1:T(1,128)S(1)} %reshape.33, f32[256,1]{0,1:T(1,128)S(1)} %bitcast.26), channel_id=1, replica_groups=mesh['tok'=4,'voc'=64] {'voc'}, use_global_device_ids=true, to_apply=%region_5.0 | all-reduce | flops 512 | bytes 4096 | tf_op jit(solution)/shard_map/pmax | solution.py:14
  339.7 0.5 broadcast.7
  340.2 0.7 reduce.6
  340.8 0.1 sub.50
  340.9 1.0 exponential_reduce_fusion
  341.9 0.1 broadcast_in_dim.13
  342.0 2.0 exponential_reduce_fusion.1
  344.0 158.6 %all-reduce = (f32[256,1]{0,1:T(1,128)S(1)}, f32[256,1]{0,1:T(1,128)S(1)}) all-reduce(f32[256,1]{0,1:T(1,128)S(1)} %broadcast_in_dim.13, f32[256,1]{0,1:T(1,128)S(1)} %bitcast.22), channel_id=1, replica_groups=mesh['tok'=4,'voc'=64] {'voc'}, use_global_device_ids=true, to_apply=%region_7.0 | all-reduce | flops 512 | bytes 4096 | tf_op jit(solution)/shard_map/psum | solution.py:15
  502.6 3.0 multiply_convert_fusion
  505.6 9.1 fusion.2
  514.7 0.0 reduce-scatter.5.cloned.1.call-update
  514.8 0.0 reduce-scatter.7.cloned.1.call-start
  514.8 7.4 fusion
  522.2 20.3 %copy.12 = bf16[3584,2048]{1,0:T(8,128)(2,1)} copy(bf16[3584,2048]{0,1:T(8,128)(2,1)} %fusion) | data formatting | bytes 29360128
  542.6 0.0 reduce-scatter.7.cloned.1.call-update
  542.6 362.8 %reduce-scatter.5.cloned.1.call-done = f32[256,56]{0,1:T(8,128)} async-done(((f32[256,3584]{0,1:T(8,128)}), f32[256,56]{0,1:T(8,128)}) %reduce-scatter.5.cloned.1.call-update) | async-done | bytes 57360 | tf_op jit(solution)/shard_map/reduce_scatter | solution.py:26
  905.4 1.4 convert_element_type.25
  906.8 177.3 %reduce-scatter.7.cloned.1.call-done = bf16[896,2048]{1,0:T(8,128)(2,1)} async-done(((bf16[3584,2048]{1,0:T(8,128)(2,1)}), bf16[896,2048]{1,0:T(8,128)(2,1)}) %reduce-scatter.7.cloned.1.call-update) | async-done | bytes 3670032
  (2 shorter events, 0.0 us)
Async XLA Ops:
  7.2 158.1 %copy-start = (bf16[256,3584]{1,0:T(8,128)(2,1)S(1)}, bf16[256,3584]{1,0:T(8,128)(2,1)}, u32[]{:S(2)}) copy-start(bf16[256,3584]{1,0:T(8,128)(2,1)} %param.4) | copy-start | bytes 5505028
  7.2 15.9 %copy-start.1 = (f32[256]{0:T(256)S(1)}, f32[256]{0:T(256)}, u32[]{:S(2)}) copy-start(f32[256]{0:T(256)} %param.7) | copy-start | bytes 3076
  7.2 158.1 %all-gather.2.cloned.1.call-start = ((), (), s32[]{:S(2)}) async-start(), calls=%async_computation.3 | async-start | bytes 18350080 | tf_op jit(solution)/shard_map/all_gather | solution.py:10
  7.9 48.8 %all-to-all-start = ((bf16[4,64,2048]{2,0,1:T(4,128)(2,1)}), bf16[4,64,2048]{2,0,1:T(4,128)(2,1)S(1)}, u32[]{:S(2)}, u32[]{:S(2)}) async-start(bf16[4,64,2048]{2,0,1:T(4,128)(2,1)} %bitcast.21), calls=%async_computation | async-start | bytes 2097152 | tf_op jit(solution)/shard_map/all_to_all | solution.py:11
  23.1 882.3 %reduce-scatter.5.cloned.1.call-start = ((), (), s32[]{:S(2)}) async-start(), calls=%async_computation.4 | async-start | bytes 3727360 | tf_op jit(solution)/shard_map/reduce_scatter | solution.py:26
  514.8 569.3 %reduce-scatter.7.cloned.1.call-start = ((), (), s32[]{:S(2)}) async-start(), calls=%async_computation.5 | async-start | bytes 18350080
Sparse Core Ops, SparseCore 0:
  9.8 155.4 all-gather.1
  514.9 390.4 reduce-scatter.4
  908.7 175.2 reduce-scatter.6
where the time goes:
time: 1090 us
  waiting for transfers between devices  678 us (62%)
  blocking collectives  324 us (30%)
  matrix products  25.4 us (2%)
  local copies, waits for them, and re-layouts  24.2 us (2%)
  starting transfers between devices  15.2 us (1%)
  between operations  13.8 us (1%)
    reduce_scatter x1, waiting for transfers between devices, body(): lax.psum_scatter(partial_hidden, 'voc', scatter_dimension=1, tiled=True)  363 us
    unnamed x4, waiting for transfers between devices  178 us
    pmax x1, blocking collectives, body(): teacher_top = lax.pmax(jnp.max(teacher, axis=1, keepdims=True), 'voc')  165 us
    psum x1, blocking collectives, body(): lax.psum(jnp.sum(jnp.exp(teacher - teacher_top), axis=1, keepdims=True),...  159 us
    all_gather x1, waiting for transfers between devices, body(): head_full = lax.all_gather(student_head, 'tok', axis=0, tiled=True)  103 us
    all_to_all x1, waiting for transfers between devices, body(): lax.all_to_all(teacher_logits, 'voc', split_axis=1, concat_axis=0, tiled=...  33.6 us
  transfers between devices with their start and end apart: 4, of which 4 were waited for; matrix products, arithmetic and copies ran while one was open for 3% of the time, Pallas kernels for 0%

commit v1 on v0

v1 whole, which is shorter than its diff:
```python
import functools

import jax
import jax.numpy as jnp
from jax import lax
from jax.experimental import pallas as pl
from jax.experimental.pallas import tpu as pltpu
from jax.sharding import PartitionSpec as P

MESH = pl.DeviceIdType.MESH
LOSS_SCALE = 64.0
D = 3584
DS = 896
TOK = 1024
TG = 256
COLS = 512
BLK = 128
NB = 8
ROWS = 56
CHUNKS = ((0, 256), (256, 256), (512, 256), (768, 128))
F32 = jnp.float32
BF16 = jnp.bfloat16


def mult(x, m):
    return pl.multiple_of(x, m)


def kernel(
    hid, head, teach, qual, hg, gh,
    hid_all, headv, hcols, tloc, ta, tb, stu, gs, hid_t, acc, stage,
    pb, r1, s1, r2, s2, fin, msg_a, got_a, msg_b, got_b, planes,
    loc, head_s, head_r, hid_s, hid_r, bc_s, bc_r, ta_s, ta_r, tb_s, tb_r,
    la_s, la_r, lb_s, lb_r, g_s, g_r, r1_s, r1_r, r2_s, r2_r, f_s, f_r, out_s,
):
    t = lax.axis_index("tok")
    v = lax.axis_index("voc")
    z = v // 16
    p = v % 16
    y = p // 4
    x = p % 4
    c = t // 2
    h = t % 2
    sib = c * 2 + (1 - h)
    cross = (1 - c) * 2 + h
    diag = (1 - c) * 2 + (1 - h)
    tz = t * 4 + z

    def plane_peer(k):
        return (t, z * 16 + lax.rem(p + k, 16))

    def tz_peer(k):
        q = lax.rem(tz + k, 16)
        return (q // 4, (q % 4) * 16 + p)

    def remote(src, dst, ss, rs, dev):
        return pltpu.make_async_remote_copy(
            src_ref=src, dst_ref=dst, send_sem=ss, recv_sem=rs, device_id=dev, device_id_type=MESH
        )

    def arrived(ref, sem):
        pltpu.make_async_copy(ref, ref, sem).wait()

    bar = pltpu.get_barrier_semaphore()

    def greet(k, _):
        pl.semaphore_signal(bar, inc=1, device_id=plane_peer(k), device_id_type=MESH)
        pl.semaphore_signal(bar, inc=1, device_id=tz_peer(k), device_id_type=MESH)
        return 0

    lax.fori_loop(1, 16, greet, 0)

    c_own = pltpu.make_async_copy(head.at[:, pl.ds(mult(COLS * t, COLS), COLS)], hcols.at[t], loc.at[0])
    c_hid = pltpu.make_async_copy(hid, hid_all.at[pl.ds(mult(TG * t, TG), TG)], loc.at[1])
    c_head = pltpu.make_async_copy(head, headv, loc.at[2])
    c_tl = pltpu.make_async_copy(teach, tloc, loc.at[3])
    c_ta = pltpu.make_async_copy(teach.at[:, p], ta.at[p // 2, p % 2], loc.at[4])
    for cp in (c_hid, c_own, c_tl, c_ta, c_head):
        cp.start()

    pl.semaphore_wait(bar, 30)

    def piece(group, q):
        return (
            pl.ds(mult(TG * group + 16 * (q // 2), 16), 16),
            pl.ds(mult(1792 * (q % 2), 128), 1792),
        )

    pr, pc = piece(0, p)
    mr, mc = piece(t, p)
    h_cross = remote(hid.at[pr, pc], hid_all.at[mr, mc], hid_s.at[0], hid_r.at[0], (cross, v))
    h_cross.start()
    znb = lax.rem(z + 2 * c + 3, 4)
    h_pair = remote(
        hid.at[pl.ds(128, 128)], hid_all.at[pl.ds(mult(TG * t + 128, 128), 128)],
        hid_s.at[1], hid_r.at[1], (cross, znb * 16 + p),
    )
    h_sib = remote(
        hid, hid_all.at[pl.ds(mult(TG * t, TG), TG)], hid_s.at[2], hid_r.at[2], (sib, v)
    )
    heads = []
    for i, (r0, rn) in enumerate(CHUNKS):
        for j, dev in enumerate((cross, diag, sib)):
            heads.append(
                remote(
                    head.at[pl.ds(r0, rn), pl.ds(mult(COLS * dev, COLS), COLS)],
                    hcols.at[t, pl.ds(r0, rn)],
                    head_s.at[i, j], head_r.at[t, i], (dev, v),
                )
            )
    for cp in heads[:3]:
        cp.start()
    h_pair.start()
    h_sib.start()
    for cp in heads[3:]:
        cp.start()

    xr, xc = piece(cross, p)
    arrived(hid_all.at[xr, xc], hid_r.at[0])

    def spread_copy(k):
        return remote(
            hid_all.at[xr, xc], hid_all.at[xr, xc], bc_s.at[k - 1], bc_r.at[k - 1], plane_peer(k)
        )

    def ta_copy(k):
        q = lax.rem(p + k, 16)
        return remote(
            teach.at[:, q], ta.at[p // 2, p % 2], ta_s.at[k - 1], ta_r.at[k - 1], plane_peer(k)
        )

    def start_spread(k, _):
        spread_copy(k).start()
        return 0

    def start_ta(k, _):
        ta_copy(k).start()
        return 0

    lax.fori_loop(1, 16, start_spread, 0)
    lax.fori_loop(1, 16, start_ta, 0)

    c_tl.wait()

    def tl_tile(i):
        return tloc[i // 4, pl.ds(mult((i % 4) * 4, 4), 4)].astype(F32)

    def top_step(i, m):
        return jnp.maximum(m, jnp.max(tl_tile(i), axis=(0, 1)))

    top16 = lax.fori_loop(0, 16, top_step, jnp.full((16, 128), -jnp.inf, F32))
    top16 = jnp.max(top16, axis=1, keepdims=True)
    top4 = jnp.maximum(jnp.maximum(top16[0:4], top16[4:8]), jnp.maximum(top16[8:12], top16[12:16]))
    top16 = jnp.concatenate([top4] * 4, axis=0)
    top_full = jnp.broadcast_to(top16, (16, 128))

    def sum_step(i, s):
        return s + jnp.sum(jnp.exp(tl_tile(i) - top_full), axis=(0, 1))

    sum16 = lax.fori_loop(0, 16, sum_step, jnp.zeros((16, 128), F32))
    sum16 = jnp.sum(sum16, axis=1, keepdims=True)
    sum4 = sum16[0:4] + sum16[4:8] + sum16[8:12] + sum16[12:16]
    lse4 = top4 + jnp.log(sum4)
    row = lax.broadcasted_iota(jnp.int32, (8, 128), 0)
    lane = lax.broadcasted_iota(jnp.int32, (8, 128), 1)
    tplane = jnp.zeros((8, 128), F32)
    for r in range(4):
        here = (row == 2 * t + v // 32) & (lane == 4 * lax.rem(v, 32) + r)
        tplane = jnp.where(here, jnp.broadcast_to(lse4[r : r + 1], (8, 128)), tplane)
    msg_a[2] = tplane

    gx = mult(TG * cross, TG)

    def wait_spread(k, _):
        ar, ac = piece(cross, lax.rem(p + 16 - k, 16))
        arrived(hid_all.at[ar, ac], bc_r.at[k - 1])
        return 0

    lax.fori_loop(1, 16, wait_spread, 0)
    fwd1 = remote(
        hid_all.at[pl.ds(gx, 128)], hid_all.at[pl.ds(gx, 128)], hid_s.at[3], hid_r.at[3], (sib, v)
    )
    fwd1.start()
    gx2 = mult(TG * cross + 128, 128)
    arrived(hid_all.at[pl.ds(gx2, 128)], hid_r.at[1])
    fwd2 = remote(
        hid_all.at[pl.ds(gx2, 128)], hid_all.at[pl.ds(gx2, 128)], hid_s.at[4], hid_r.at[4], (sib, v)
    )
    fwd2.start()
    c_hid.wait()
    arrived(hid_all.at[pl.ds(mult(TG * sib, TG), TG)], hid_r.at[2])
    arrived(hid_all.at[pl.ds(mult(TG * diag, 128), 128)], hid_r.at[3])
    arrived(hid_all.at[pl.ds(mult(TG * diag + 128, 128), 128)], hid_r.at[4])

    def multiply(slot, r0, rn, first):
        base = mult(DS * slot + r0, 128)

        def step(m, _):
            rows = pl.ds(mult(m * 256, 256), 256)
            term = jnp.dot(
                hid_all[rows, pl.ds(base, rn)], hcols[slot, pl.ds(r0, rn), :],
                preferred_element_type=F32,
            )
            if first:
                stu[rows, :] = term
            else:
                stu[rows, :] += term
            return 0

        lax.fori_loop(0, 4, step, 0)

    def wait_head(slot, i):
        r0, rn = CHUNKS[i]
        arrived(hcols.at[slot, pl.ds(r0, rn)], head_r.at[slot, i])

    c_own.wait()
    multiply(t, 0, DS, True)
    for i in range(4):
        wait_head(sib, i)
    multiply(sib, 0, DS, False)

    def turn(i, _):
        rows = pl.ds(mult(i * 128, 128), 128)
        for j in range(7):
            block = hid_all[rows, pl.ds(mult(DS * t + 128 * j, 128), 128)]
            hid_t[128 * j : 128 * (j + 1), rows] = block.astype(F32).T.astype(BF16)
        return 0

    lax.fori_loop(0, 8, turn, 0)

    for i in range(3):
        r0, rn = CHUNKS[i]
        wait_head(cross, i)
        multiply(cross, r0, rn, False)
        wait_head(diag, i)
        multiply(diag, r0, rn, False)

    c_ta.wait()

    def wait_ta(k, _):
        q = lax.rem(p + 16 - k, 16)
        arrived(ta.at[q // 2, q % 2], ta_r.at[k - 1])
        return 0

    lax.fori_loop(1, 16, wait_ta, 0)
    wait_head(cross, 3)
    wait_head(diag, 3)
    for cp in heads:
        cp.wait_send()

    def tb_copy(k):
        q = lax.rem(tz + k, 16)
        return remote(
            ta.at[:, :, q % 4, q // 4], tb.at[tz], tb_s.at[k], tb_r.at[tz], tz_peer(k)
        )

    def start_tb(k, _):
        tb_copy(k).start()
        return 0

    lax.fori_loop(1, 16, start_tb, 0)
    c_tb = pltpu.make_async_copy(ta.at[:, :, z, t], tb.at[tz], tb_r.at[tz])
    c_tb.start()

    r0, rn = CHUNKS[3]
    multiply(cross, r0, rn, False)
    multiply(diag, r0, rn, False)

    def stats(b, _):
        rows = pl.ds(mult(b * BLK, BLK), BLK)
        val = stu[rows, :]
        top = jnp.max(val, axis=1, keepdims=True)
        e = jnp.exp(val - top)
        stu[rows, :] = e
        tot = jnp.sum(e, axis=1, keepdims=True)
        msg_a[0, pl.ds(b, 1), :] = jnp.broadcast_to(top, (BLK, BLK)).T[0:1, :]
        msg_a[1, pl.ds(b, 1), :] = jnp.broadcast_to(tot, (BLK, BLK)).T[0:1, :]
        return 0

    lax.fori_loop(0, NB, stats, 0)

    def la_copy(k):
        return remote(msg_a, got_a.at[k - 1], la_s.at[k - 1], la_r.at[k - 1], plane_peer(k))

    def lb_copy(k):
        return remote(msg_b, got_b.at[k - 1], lb_s.at[k - 1], lb_r.at[k - 1], tz_peer(k))

    def start_la(k, _):
        la_copy(k).start()
        return 0

    def start_lb(k, _):
        lb_copy(k).start()
        return 0

    def combine(msg, got):
        top = jnp.maximum(msg[0], jnp.max(got[:, 0], axis=0))
        tot = msg[1] * jnp.exp(msg[0] - top) + jnp.sum(
            got[:, 1] * jnp.exp(got[:, 0] - top[None]), axis=0
        )
        return top, tot, msg[2] + jnp.sum(got[:, 2], axis=0)

    lax.fori_loop(1, 16, start_la, 0)

    def wait_la(k, _):
        arrived(got_a.at[k - 1], la_r.at[k - 1])
        return 0

    lax.fori_loop(1, 16, wait_la, 0)
    top, tot, tlse = combine(msg_a, got_a)
    msg_b[0] = top
    msg_b[1] = tot
    msg_b[2] = tlse
    q2 = qual[...]
    qplane = jnp.where(row == 2 * t, jnp.broadcast_to(q2[0:1], (8, 128)), 0.0)
    msg_b[3] = jnp.where(row == 2 * t + 1, jnp.broadcast_to(q2[1:2], (8, 128)), qplane)
    lax.fori_loop(1, 16, start_lb, 0)

    def wait_lb(k, _):
        arrived(got_b.at[k - 1], lb_r.at[k - 1])
        return 0

    lax.fori_loop(1, 16, wait_lb, 0)
    top, tot, tlse = combine(msg_b, got_b)
    weight = (msg_b[3] + jnp.sum(got_b[:, 3], axis=0)) * (0.25 * LOSS_SCALE)
    planes[0] = weight * jnp.exp(msg_a[0] - top) / tot
    planes[1] = tlse - jnp.log(weight)

    def g_cross(b):
        at = (pl.ds(mult(b * BLK, BLK), BLK), pl.ds(mult(COLS * t, COLS), COLS))
        return remote(gs.at[at], gs.at[at], g_s.at[b, 0], g_r.at[b, 0], (cross, v))

    def g_sib(b):
        at = (pl.ds(mult(b * BLK, BLK), BLK), pl.ds(mult(COLS * t, COLS), COLS))
        return remote(gs.at[at], gs.at[at], g_s.at[b, 1], g_r.at[b, 1], (sib, v))

    def g_fwd(b):
        at = (pl.ds(mult(b * BLK, BLK), BLK), pl.ds(mult(COLS * cross, COLS), COLS))
        return remote(gs.at[at], gs.at[at], g_s.at[b, 2], g_r.at[b, 2], (sib, v))

    sub = lax.broadcasted_iota(jnp.int32, (16, 8, 128), 1) < 4

    def make_grads(b, _):
        rows = pl.ds(mult(b * BLK, BLK), BLK)
        for s in range(2):
            arrived(tb.at[2 * b + s], tb_r.at[2 * b + s])
        even = tb[pl.ds(mult(2 * b, 2), 2), :, 0].astype(F32).reshape(16, 16, 128)
        odd = tb[pl.ds(mult(2 * b, 2), 2), :, 1].astype(F32).reshape(16, 16, 128)
        scale = jnp.broadcast_to(planes[0, pl.ds(b, 1), :], (BLK, BLK)).T
        tl = jnp.broadcast_to(planes[1, pl.ds(b, 1), :], (BLK, BLK)).T
        for q in range(4):
            half = slice(8 * (q // 2), 8 * (q // 2) + 8)
            lo, hi = even[:, half], odd[:, half]
            if q % 2 == 0:
                mixed = jnp.where(sub, lo, pltpu.roll(hi, 4, 1))
            else:
                mixed = jnp.where(sub, pltpu.roll(lo, 4, 1), hi)
            teacher = mixed.reshape(BLK, 128)
            e = stu[rows, 128 * q : 128 * (q + 1)]
            g = e * scale - jnp.exp(teacher - tl)
            gs[rows, pl.ds(mult(COLS * t + 128 * q, 128), 128)] = g.astype(BF16)
        g_cross(b).start()
        g_sib(b).start()
        return 0

    lax.fori_loop(0, NB, make_grads, 0)
    c_head.wait()

    def line_peer(first, k):
        if first == 0:
            return (t, z * 16 + y * 4 + lax.rem(x + k, 4))
        return (t, z * 16 + lax.rem(y + k, 4) * 4 + x)

    def part1(b, par, k):
        if par == 0:
            return pb.at[b, :, lax.rem(x + k, 4)]
        return pb.at[b, lax.rem(y + k, 4)]

    def copy1(b, par, k):
        return remote(
            part1(b, par, k), r1.at[b, k - 1], r1_s.at[b, k - 1], r1_r.at[b, k - 1], line_peer(par, k)
        )

    def copy2(b, par, k):
        to = lax.rem(y + k, 4) if par == 0 else lax.rem(x + k, 4)
        return remote(
            s1.at[b, to], r2.at[b, k - 1], r2_s.at[b, k - 1], r2_r.at[b, k - 1], line_peer(1 - par, k)
        )

    def copy3(b):
        return remote(
            s2.at[b], fin.at[z, lax.rem(b, 2)], f_s.at[b], f_r.at[z, lax.rem(b, 2)], (b // 2, t * 16 + p)
        )

    def mine(b):
        return (b // 2 == t) & (t == z)

    def step1(b, par):
        rows = pl.ds(mult(b * BLK, BLK), BLK)
        arrived(gs.at[rows, pl.ds(mult(COLS * cross, COLS), COLS)], g_r.at[b, 0])
        g_fwd(b).start()
        arrived(gs.at[rows, pl.ds(mult(COLS * sib, COLS), COLS)], g_r.at[b, 1])
        arrived(gs.at[rows, pl.ds(mult(COLS * diag, COLS), COLS)], g_r.at[b, 2])
        part = lax.dot_general(
            headv[...], gs[rows, :], (((1,), (1,)), ((), ())), preferred_element_type=F32
        )
        pb[b] = part.reshape(4, 4, ROWS, BLK)
        for k in (2, 1, 3):
            copy1(b, par, k).start()

    def step2(b, par):
        for k in (1, 2, 3):
            arrived(r1.at[b, k - 1], r1_r.at[b, k - 1])
        own = pb[b, :, x] if par == 0 else pb[b, y]
        s1[b] = (own + r1[b, 0]) + (r1[b, 1] + r1[b, 2])
        for k in (2, 1, 3):
            copy2(b, par, k).start()

    def step3(b, par):
        for k in (1, 2, 3):
            arrived(r2.at[b, k - 1], r2_r.at[b, k - 1])
        own = s1[b, y] if par == 0 else s1[b, x]
        total = (own + r2[b, 0]) + (r2[b, 1] + r2[b, 2])
        s2[b] = total

        @pl.when(mine(b))
        def _():
            fin[z, lax.rem(b, 2)] = total

        @pl.when(jnp.logical_not(mine(b)))
        def _():
            copy3(b).start()

    def group_term(g, i):
        term = jnp.dot(
            hid_t[128 * i : 128 * (i + 1), pl.ds(mult(g * TG, TG), TG)],
            gs[pl.ds(mult(g * TG, TG), TG), :],
            preferred_element_type=F32,
        )
        return term.astype(BF16).astype(F32)

    def group(g, _):
        b0, b1 = 2 * g, 2 * g + 1
        step1(b0, 0)

        @pl.when(g > 0)
        def _():
            step2(b0 - 1, 1)
            step3(b0 - 2, 0)

        step1(b1, 1)
        step2(b0, 0)

        @pl.when(g > 0)
        def _():
            step3(b0 - 1, 1)

        @pl.when(g == 0)
        def _():
            for i in range(7):
                acc[128 * i : 128 * (i + 1), :] = group_term(g, i)

        @pl.when((g > 0) & (g < 3))
        def _():
            for i in range(7):
                acc[128 * i : 128 * (i + 1), :] += group_term(g, i)

        return 0

    lax.fori_loop(0, 4, group, 0)
    step2(7, 1)
    outs = []
    for i in range(7):
        rows = slice(128 * i, 128 * (i + 1))
        stage[rows, :] = (acc[rows, :] + group_term(3, i)).astype(BF16)
        cp = pltpu.make_async_copy(stage.at[pl.ds(128 * i, 128)], gh.at[pl.ds(128 * i, 128)], out_s.at[i])
        cp.start()
        outs.append(cp)
    step3(6, 0)
    step3(7, 1)

    for s in range(2):
        for k in range(4):

            @pl.when(jnp.logical_not((t == z) & (z == k)))
            def _():
                arrived(fin.at[k, s], f_r.at[k, s])

        hg[:, 128 * s : 128 * (s + 1)] = (
            (fin[0, s] + fin[1, s]) + (fin[2, s] + fin[3, s])
        ).astype(BF16)

    for cp in (h_cross, h_pair, h_sib, fwd1, fwd2):
        cp.wait_send()

    def drain(k, _):
        spread_copy(k).wait_send()
        ta_copy(k).wait_send()
        tb_copy(k).wait_send()
        la_copy(k).wait_send()
        lb_copy(k).wait_send()
        return 0

    lax.fori_loop(1, 16, drain, 0)

    def drain_blocks(g, _):
        for par in range(2):
            b = 2 * g + par
            g_cross(b).wait_send()
            g_sib(b).wait_send()
            g_fwd(b).wait_send()
            for k in (1, 2, 3):
                copy1(b, par, k).wait_send()
                copy2(b, par, k).wait_send()

            @pl.when(jnp.logical_not(mine(b)))
            def _():
                copy3(b).wait_send()

        return 0

    lax.fori_loop(0, 4, drain_blocks, 0)
    for cp in outs:
        cp.wait()


def body(hidden_states, student_head, teacher_logits, quality):
    teach = (
        teacher_logits.reshape(4, 256, 4, 128).transpose(1, 2, 0, 3).reshape(4, 16, 4, 16, 128)
    )
    any_ = pl.BlockSpec(memory_space=pl.ANY)
    vmem = pl.BlockSpec(memory_space=pltpu.VMEM)
    dma = pltpu.SemaphoreType.DMA
    hg, gh = pl.pallas_call(
        kernel,
        name="distill_backward",
        out_shape=(
            jax.ShapeDtypeStruct((ROWS, TG), BF16),
            jax.ShapeDtypeStruct((DS, 2048), BF16),
        ),
        in_specs=[any_, any_, any_, vmem],
        out_specs=(vmem, any_),
        scratch_shapes=[
            pltpu.VMEM((TOK, D), BF16),
            pltpu.VMEM((DS, 2048), BF16),
            pltpu.VMEM((4, DS, COLS), BF16),
            pltpu.VMEM((4, 16, 4, 16, 128), BF16),
            pltpu.VMEM((8, 2, 4, 4, 16, 128), BF16),
            pltpu.VMEM((16, 8, 2, 16, 128), BF16),
            pltpu.VMEM((TOK, COLS), F32),
            pltpu.VMEM((TOK, 2048), BF16),
            pltpu.VMEM((DS, TOK), BF16),
            pltpu.VMEM((DS, 2048), F32),
            pltpu.VMEM((DS, 2048), BF16),
            pltpu.VMEM((NB, 4, 4, ROWS, BLK), F32),
            pltpu.VMEM((NB, 3, 4, ROWS, BLK), F32),
            pltpu.VMEM((NB, 4, ROWS, BLK), F32),
            pltpu.VMEM((NB, 3, ROWS, BLK), F32),
            pltpu.VMEM((NB, ROWS, BLK), F32),
            pltpu.VMEM((4, 2, ROWS, BLK), F32),
            pltpu.VMEM((3, 8, 128), F32),
            pltpu.VMEM((15, 3, 8, 128), F32),
            pltpu.VMEM((4, 8, 128), F32),
            pltpu.VMEM((15, 4, 8, 128), F32),
            pltpu.VMEM((2, 8, 128), F32),
            dma((5,)),
            dma((4, 3)), dma((4, 4)),
            dma((5,)), dma((5,)),
            dma((15,)), dma((15,)),
            dma((15,)), dma((15,)),
            dma((16,)), dma((16,)),
            dma((15,)), dma((15,)),
            dma((15,)), dma((15,)),
            dma((NB, 3)), dma((NB, 3)),
            dma((NB, 3)), dma((NB, 3)),
            dma((NB, 3)), dma((NB, 3)),
            dma((NB,)), dma((4, 2)),
            dma((7,)),
        ],
        compiler_params=pltpu.CompilerParams(
            collective_id=0, has_side_effects=True, vmem_limit_bytes=60 * 2**20
        ),
        cost_estimate=pl.CostEstimate(
            flops=3 * 2 * TOK * DS * 2048, bytes_accessed=15 * 2**20, transcendentals=2**21
        ),
    )(hidden_states, student_head, teach, quality.reshape(2, 128))
    return hg.T, gh


def solution(mesh):
    return jax.shard_map(
        body,
        mesh=mesh,
        in_specs=(P("tok", None), P("tok", "voc"), P(("tok", "voc"), None), P("tok")),
        out_specs=(P("tok", "voc"), P("tok", "voc")),
        check_vma=False,
    )
```

time: 1090 us -> 158 us (0.14)
  the two profiles are of different devices: /device:TPU:1 before, /device:TPU:33 now
where the time goes in v1:
time: 158 us
  Pallas kernels  152 us (96%)
  local copies, waits for them, and re-layouts  5.73 us (4%)
    pallas_call x1, Pallas kernels, body(): pl.pallas_call(kernel, name='distill_backward', out_shape=(jax.ShapeDtype...  152 us
    unnamed x2, local copies, waits for them, and re-layouts  5.73 us

profile of v1, /device:TPU:33, one launch (start us, length us, event | category | flops | bytes accessed | tf_op | source)
XLA Modules:
  0.0 158.1 jit_solution(3594293855291327126)
XLA Ops:
  0.6 151.8 %distill_backward.1 = (bf16[56,256]{1,0:T(8,128)(2,1)}, bf16[896,2048]{1,0:T(8,128)(2,1)}) custom-call(bf16[256,3584]{1,0:T(8,128)(2,1)} %hid.1, bf16[896,2048]{1,0:T(8,128)(2,1)} %head.1, bf16[4,16,4,16,128]{4,3,2,1,0:T(8,128)(2,1)} %bitcast.8, f32[2,128]{1,0:T(2,128)} %bitcast.9), custom_call_target="tpu_custom_call" | custom-call | flops 11274289152 | bytes 15728640 | tf_op jit(solution)/shard_map/distill_backward/pallas_call | solution.py:534
  152.4 1.4 copy.9
  153.8 4.4 %copy.10 = bf16[896,2048]{1,0:T(8,128)(2,1)} copy(bf16[896,2048]{1,0:T(8,128)(2,1)} %get-tuple-element.9) | data formatting | bytes 7340032

commit v2 on v1

v2 whole, which is shorter than its diff:
```python
import functools

import jax
import jax.numpy as jnp
from jax import lax
from jax.experimental import pallas as pl
from jax.experimental.pallas import tpu as pltpu
from jax.sharding import PartitionSpec as P

MESH = pl.DeviceIdType.MESH
LOSS_SCALE = 64.0
D = 3584
DS = 896
TOK = 1024
TG = 256
COLS = 512
BLK = 128
TB_SPLIT = 8
NB = 8
ROWS = 56
CHUNKS = ((0, 256), (256, 256), (512, 256), (768, 128))
F32 = jnp.float32
BF16 = jnp.bfloat16


def mult(x, m):
    return pl.multiple_of(x, m)


def kernel(
    hid, head, teach, qual, hg, gh,
    hid_all, headv, hcols, tloc, ta, tb, stu, gs, hid_t, acc,
    pb, ax, ay, r1x, r1y, s1x, s1y, r2x, r2y, s2, fin,
    row_a, got_t, tq, st, got_a, row_b, got_b, full, scale,
    loc, head_s, head_r, hid_s, hid_r, bc_s, bc_r, ta_s, ta_r, tb_s, tb_r,
    t1_s, t1_r, t2_s, t2_r, la_s, la_r, lb_s, lb_r, lc_s, lc_r, g_s, g_r,
    ax_s, ax_r, ay_s, ay_r, r1x_s, r1x_r, r1y_s, r1y_r, r2x_s, r2x_r, r2y_s, r2y_r, f_s, f_r,
):
    t = lax.axis_index("tok")
    v = lax.axis_index("voc")
    z = v // 16
    p = v % 16
    y = p // 4
    x = p % 4
    c = t // 2
    h = t % 2
    sib = c * 2 + (1 - h)
    cross = (1 - c) * 2 + h
    diag = (1 - c) * 2 + (1 - h)
    tz = t * 4 + z

    def plane_peer(k):
        return (t, z * 16 + lax.rem(p + k, 16))

    def tz_peer(k):
        q = lax.rem(tz + k, 16)
        return (q // 4, (q % 4) * 16 + p)

    def remote(src, dst, ss, rs, dev):
        return pltpu.make_async_remote_copy(
            src_ref=src, dst_ref=dst, send_sem=ss, recv_sem=rs, device_id=dev, device_id_type=MESH
        )

    def arrived(ref, sem):
        pltpu.make_async_copy(ref, ref, sem).wait()

    bar = pltpu.get_barrier_semaphore()

    def greet(k, _):
        pl.semaphore_signal(bar, inc=1, device_id=plane_peer(k), device_id_type=MESH)
        pl.semaphore_signal(bar, inc=1, device_id=tz_peer(k), device_id_type=MESH)
        return 0

    lax.fori_loop(1, 16, greet, 0)

    c_own = pltpu.make_async_copy(head.at[:, pl.ds(mult(COLS * t, COLS), COLS)], hcols.at[t], loc.at[0])
    c_hid = pltpu.make_async_copy(hid, hid_all.at[pl.ds(mult(TG * t, TG), TG)], loc.at[1])
    order = (t, sib, cross, diag)
    c_heads = [
        pltpu.make_async_copy(
            head.at[:, pl.ds(mult(COLS * dev, COLS), COLS)], headv.at[:, pl.ds(COLS * j, COLS)], loc.at[5 + j]
        )
        for j, dev in enumerate(order)
    ]
    c_tl = pltpu.make_async_copy(teach, tloc, loc.at[3])
    c_ta = pltpu.make_async_copy(teach.at[:, p], ta.at[p // 2, p % 2], loc.at[4])
    for cp in (c_hid, c_own, c_tl, c_ta, *c_heads):
        cp.start()

    pl.semaphore_wait(bar, 30)

    def piece(group, q):
        return (
            pl.ds(mult(TG * group + 16 * (q // 2), 16), 16),
            pl.ds(mult(1792 * (q % 2), 128), 1792),
        )

    pr, pc = piece(0, p)
    mr, mc = piece(t, p)
    h_cross = remote(hid.at[pr, pc], hid_all.at[mr, mc], hid_s.at[0], hid_r.at[0], (cross, v))
    h_cross.start()
    znb = lax.rem(z + 2 * c + 3, 4)
    h_pair = remote(
        hid.at[pl.ds(128, 128)], hid_all.at[pl.ds(mult(TG * t + 128, 128), 128)],
        hid_s.at[1], hid_r.at[1], (cross, znb * 16 + p),
    )
    h_sib = remote(
        hid, hid_all.at[pl.ds(mult(TG * t, TG), TG)], hid_s.at[2], hid_r.at[2], (sib, v)
    )
    heads = []
    for i, (r0, rn) in enumerate(CHUNKS):
        for j, dev in enumerate((cross, diag, sib)):
            heads.append(
                remote(
                    head.at[pl.ds(r0, rn), pl.ds(mult(COLS * dev, COLS), COLS)],
                    hcols.at[t, pl.ds(r0, rn)],
                    head_s.at[i, j], head_r.at[t, i], (dev, v),
                )
            )
    for cp in heads[:3]:
        cp.start()
    h_pair.start()
    h_sib.start()
    for cp in heads[3:]:
        cp.start()

    xr, xc = piece(cross, p)
    arrived(hid_all.at[xr, xc], hid_r.at[0])

    def spread_copy(k):
        return remote(
            hid_all.at[xr, xc], hid_all.at[xr, xc], bc_s.at[k - 1], bc_r.at[k - 1], plane_peer(k)
        )

    def ta_copy(k):
        q = lax.rem(p + k, 16)
        return remote(
            teach.at[:, q], ta.at[p // 2, p % 2], ta_s.at[k - 1], ta_r.at[k - 1], plane_peer(k)
        )

    def start_spread(k, _):
        spread_copy(k).start()
        return 0

    def start_ta(k, _):
        ta_copy(k).start()
        return 0

    lax.fori_loop(1, 16, start_spread, 0)
    lax.fori_loop(1, 16, start_ta, 0)

    c_tl.wait()

    def tl_tile(i):
        return tloc[i // 4, pl.ds(mult((i % 4) * 4, 4), 4)].astype(F32)

    def top_step(i, m):
        return jnp.maximum(m, jnp.max(tl_tile(i), axis=(0, 1)))

    top16 = lax.fori_loop(0, 16, top_step, jnp.full((16, 128), -jnp.inf, F32))
    top16 = jnp.max(top16, axis=1, keepdims=True)
    top4 = jnp.maximum(jnp.maximum(top16[0:4], top16[4:8]), jnp.maximum(top16[8:12], top16[12:16]))
    top16 = jnp.concatenate([top4] * 4, axis=0)
    top_full = jnp.broadcast_to(top16, (16, 128))

    def sum_step(i, s):
        return s + jnp.sum(jnp.exp(tl_tile(i) - top_full), axis=(0, 1))

    sum16 = lax.fori_loop(0, 16, sum_step, jnp.zeros((16, 128), F32))
    sum16 = jnp.sum(sum16, axis=1, keepdims=True)
    sum4 = sum16[0:4] + sum16[4:8] + sum16[8:12] + sum16[12:16]
    lse4 = top4 + jnp.log(sum4)
    lane = lax.broadcasted_iota(jnp.int32, (1, 128), 1)
    low = lane < 64
    trow = jnp.zeros((1, 128), F32)
    for r in range(4):
        trow = jnp.where(lane == 4 * p + r, jnp.broadcast_to(lse4[r : r + 1], (1, 128)), trow)
    row_a[...] = trow

    def swap(a):
        return pltpu.roll(a, 64, len(a.shape) - 1)

    def t1_copy(k):
        return remote(row_a, got_t.at[k - 1], t1_s.at[k - 1], t1_r.at[k - 1], plane_peer(k))

    def t2_copy(k):
        return remote(tq.at[tz], tq.at[tz], t2_s.at[k - 1], t2_r.at[k - 1], tz_peer(k))

    def start_t1(k, _):
        t1_copy(k).start()
        return 0

    def start_t2(k, _):
        t2_copy(k).start()
        return 0

    lax.fori_loop(1, 16, start_t1, 0)

    def clear(i, _):
        acc[pl.ds(mult(i * 64, 64), 64), :] = jnp.zeros((64, 2048), F32)
        return 0

    lax.fori_loop(0, 14, clear, 0)

    def wait_t1(k, _):
        arrived(got_t.at[k - 1], t1_r.at[k - 1])
        return 0

    lax.fori_loop(1, 16, wait_t1, 0)
    tl_row = row_a[...] + jnp.sum(got_t[...], axis=0)
    q_row = qual[pl.ds(z // 2, 1), :]
    weight = LOSS_SCALE * jnp.where(lax.rem(z, 2) == 0, q_row, swap(q_row))
    tq[tz] = jnp.where(low, tl_row - jnp.log(weight), swap(weight))
    lax.fori_loop(1, 16, start_t2, 0)

    gx = mult(TG * cross, TG)

    def wait_spread(k, _):
        ar, ac = piece(cross, lax.rem(p + 16 - k, 16))
        arrived(hid_all.at[ar, ac], bc_r.at[k - 1])
        return 0

    lax.fori_loop(1, 16, wait_spread, 0)
    fwd1 = remote(
        hid_all.at[pl.ds(gx, 128)], hid_all.at[pl.ds(gx, 128)], hid_s.at[3], hid_r.at[3], (sib, v)
    )
    fwd1.start()
    gx2 = mult(TG * cross + 128, 128)
    arrived(hid_all.at[pl.ds(gx2, 128)], hid_r.at[1])
    fwd2 = remote(
        hid_all.at[pl.ds(gx2, 128)], hid_all.at[pl.ds(gx2, 128)], hid_s.at[4], hid_r.at[4], (sib, v)
    )
    fwd2.start()
    c_hid.wait()
    arrived(hid_all.at[pl.ds(mult(TG * sib, TG), TG)], hid_r.at[2])
    arrived(hid_all.at[pl.ds(mult(TG * diag, 128), 128)], hid_r.at[3])
    arrived(hid_all.at[pl.ds(mult(TG * diag + 128, 128), 128)], hid_r.at[4])

    def multiply(slot, r0, rn, first):
        base = mult(DS * slot + r0, 128)

        term = jnp.dot(
            hid_all[:, pl.ds(base, rn)], hcols[slot, pl.ds(r0, rn), :], preferred_element_type=F32
        )
        if first:
            stu[...] = term
        else:
            stu[...] += term

    def wait_head(slot, i):
        r0, rn = CHUNKS[i]
        arrived(hcols.at[slot, pl.ds(r0, rn)], head_r.at[slot, i])

    c_own.wait()
    multiply(t, 0, DS, True)
    for i in range(4):
        wait_head(sib, i)
    multiply(sib, 0, DS, False)

    def turn(i, _):
        rows = pl.ds(mult(i * 128, 128), 128)
        for j in range(7):
            block = hid_all[rows, pl.ds(mult(DS * t + 128 * j, 128), 128)]
            hid_t[128 * j : 128 * (j + 1), rows] = block.astype(F32).T.astype(BF16)
        return 0

    lax.fori_loop(0, 8, turn, 0)

    for i in range(3):
        r0, rn = CHUNKS[i]
        wait_head(cross, i)
        multiply(cross, r0, rn, False)
        wait_head(diag, i)
        multiply(diag, r0, rn, False)

    c_ta.wait()

    def wait_ta(k, _):
        q = lax.rem(p + 16 - k, 16)
        arrived(ta.at[q // 2, q % 2], ta_r.at[k - 1])
        return 0

    lax.fori_loop(1, 16, wait_ta, 0)
    wait_head(cross, 3)
    wait_head(diag, 3)
    for cp in heads:
        cp.wait_send()

    def tb_copy(k):
        q = lax.rem(tz + k, 16)
        return remote(
            ta.at[:, :, q % 4, q // 4], tb.at[tz], tb_s.at[k], tb_r.at[tz], tz_peer(k)
        )

    def start_tb(k, _):
        tb_copy(k).start()
        return 0

    lax.fori_loop(1, TB_SPLIT, start_tb, 0)
    c_tb = pltpu.make_async_copy(ta.at[:, :, z, t], tb.at[tz], tb_r.at[tz])
    c_tb.start()

    r0, rn = CHUNKS[3]
    multiply(cross, r0, rn, False)
    multiply(diag, r0, rn, False)

    def stats(b, _):
        rows = pl.ds(mult(b * BLK, BLK), BLK)
        val = stu[rows, :]
        top = jnp.max(val, axis=1, keepdims=True)
        e = jnp.exp(val - top)
        stu[rows, :] = e
        tot = jnp.sum(e, axis=1, keepdims=True)
        both = jnp.where(jnp.broadcast_to(low, (BLK, BLK)), top, tot).T
        m_row, s_row = both[0:1, :], both[64:65, :]
        st[2 * b] = jnp.where(low, m_row, swap(s_row))
        st[2 * b + 1] = jnp.where(low, swap(m_row), s_row)
        return 0

    lax.fori_loop(0, NB, stats, 0)

    def la_copy(k):
        return remote(
            st.at[lax.rem(p + k, 16)], got_a.at[k - 1], la_s.at[k - 1], la_r.at[k - 1], plane_peer(k)
        )

    def lb_copy(k):
        return remote(row_b, got_b.at[k - 1], lb_s.at[k - 1], lb_r.at[k - 1], tz_peer(k))

    def lc_copy(k):
        return remote(full.at[p], full.at[p], lc_s.at[k - 1], lc_r.at[k - 1], plane_peer(k))

    def start_la(k, _):
        la_copy(k).start()
        return 0

    def start_lb(k, _):
        lb_copy(k).start()
        return 0

    def start_lc(k, _):
        lc_copy(k).start()
        return 0

    def combine(mine, got):
        top = jnp.maximum(mine, jnp.max(got, axis=0))
        tot = swap(mine) * jnp.exp(mine - top) + jnp.sum(swap(got) * jnp.exp(got - top[None]), axis=0)
        return jnp.where(low, top, swap(tot))

    lax.fori_loop(1, 16, start_la, 0)

    def wait_la(k, _):
        arrived(got_a.at[k - 1], la_r.at[k - 1])
        return 0

    lax.fori_loop(1, 16, wait_la, 0)
    row_b[...] = combine(st[p], got_a[...])
    lax.fori_loop(1, 16, start_lb, 0)
    lax.fori_loop(TB_SPLIT, 16, start_tb, 0)

    def wait_lb(k, _):
        arrived(got_b.at[k - 1], lb_r.at[k - 1])
        return 0

    lax.fori_loop(1, 16, wait_lb, 0)
    full[p] = combine(row_b[...], got_b[...])
    lax.fori_loop(1, 16, start_lc, 0)

    def wait_t2(k, _):
        q = lax.rem(tz + 16 - k, 16)
        arrived(tq.at[q], t2_r.at[k - 1])
        return 0

    def wait_lc(k, _):
        q = lax.rem(p + 16 - k, 16)
        arrived(full.at[q], lc_r.at[k - 1])
        return 0

    lax.fori_loop(1, 16, wait_t2, 0)
    lax.fori_loop(1, 16, wait_lc, 0)
    scale[...] = swap(tq[...]) * jnp.exp(st[...] - full[...]) / swap(full[...])

    def g_copy(b, j, src, dst, dev):
        rows = pl.ds(mult(b * BLK, BLK), BLK)
        return remote(
            gs.at[rows, pl.ds(COLS * src, COLS)], gs.at[rows, pl.ds(COLS * dst, COLS)],
            g_s.at[b, j], g_r.at[b, j], (dev, v),
        )

    def g_cross(b):
        return g_copy(b, 0, 0, 2, cross)

    def g_sib(b):
        return g_copy(b, 1, 0, 1, sib)

    def g_fwd(b):
        return g_copy(b, 2, 2, 3, sib)

    def g_wait(b, j):
        slot = (2, 1, 3)[j]
        rows = pl.ds(mult(b * BLK, BLK), BLK)
        arrived(gs.at[rows, pl.ds(COLS * slot, COLS)], g_r.at[b, j])

    sub = lax.broadcasted_iota(jnp.int32, (16, 8, 128), 1) < 4

    def make_grads(b, _):
        rows = pl.ds(mult(b * BLK, BLK), BLK)
        for s in range(2):
            arrived(tb.at[2 * b + s], tb_r.at[2 * b + s])
        even = tb[pl.ds(mult(2 * b, 2), 2), :, 0].astype(F32).reshape(16, 16, 128)
        odd = tb[pl.ds(mult(2 * b, 2), 2), :, 1].astype(F32).reshape(16, 16, 128)
        sc_row = jnp.where(low, scale[2 * b], swap(scale[2 * b + 1]))
        tl_row = jnp.where(low, tq[2 * b], swap(tq[2 * b + 1]))
        sc = jnp.broadcast_to(sc_row, (BLK, BLK)).T
        tl = jnp.broadcast_to(tl_row, (BLK, BLK)).T
        for q in range(4):
            half = slice(8 * (q // 2), 8 * (q // 2) + 8)
            lo, hi = even[:, half], odd[:, half]
            if q % 2 == 0:
                mixed = jnp.where(sub, lo, pltpu.roll(hi, 4, 1))
            else:
                mixed = jnp.where(sub, pltpu.roll(lo, 4, 1), hi)
            teacher = mixed.reshape(BLK, 128)
            e = stu[rows, 128 * q : 128 * (q + 1)]
            g = e * sc - jnp.exp(teacher - tl)
            gs[rows, 128 * q : 128 * (q + 1)] = g.astype(BF16)
        g_cross(b).start()
        g_sib(b).start()
        return 0

    lax.fori_loop(0, NB, make_grads, 0)
    for cp in c_heads:
        cp.wait()

    ca = x + h * (y - x)
    cb = y + h * (x - y)

    def line_a(k):
        return (t, z * 16 + (1 - h) * (y * 4 + lax.rem(x + k, 4)) + h * (lax.rem(y + k, 4) * 4 + x))

    def line_b(k):
        return (t, z * 16 + h * (y * 4 + lax.rem(x + k, 4)) + (1 - h) * (lax.rem(y + k, 4) * 4 + x))

    def copies_a(b, i):
        k = 1 + 2 * i
        return (
            remote(
                pb.at[b, pl.ds(2 * i, 2), lax.rem(ca + 2, 4), pl.ds(0, 32)], ax.at[b, i],
                ax_s.at[b, i], ax_r.at[b, i], line_a(k),
            ),
            remote(
                pb.at[b, lax.rem(cb + 2, 4), pl.ds(2 * i, 2), pl.ds(32, 24)], ay.at[b, i],
                ay_s.at[b, i], ay_r.at[b, i], line_b(k),
            ),
        )

    def copies_b(b, i):
        k = 1 + 2 * i
        return (
            remote(
                pb.at[b, :, lax.rem(ca + k, 4), pl.ds(0, 32)], r1x.at[b, i],
                r1x_s.at[b, i], r1x_r.at[b, i], line_a(k),
            ),
            remote(
                pb.at[b, lax.rem(cb + k, 4), :, pl.ds(32, 24)], r1y.at[b, i],
                r1y_s.at[b, i], r1y_r.at[b, i], line_b(k),
            ),
        )

    def copies2(b, k):
        i = k - 1
        return (
            remote(
                s1x.at[b, lax.rem(cb + k, 4)], r2x.at[b, i], r2x_s.at[b, i], r2x_r.at[b, i], line_b(k)
            ),
            remote(
                s1y.at[b, lax.rem(ca + k, 4)], r2y.at[b, i], r2y_s.at[b, i], r2y_r.at[b, i], line_a(k)
            ),
        )

    def copy3(b):
        return remote(
            s2.at[b], fin.at[z, lax.rem(b, 2)], f_s.at[b], f_r.at[z, lax.rem(b, 2)], (b // 2, t * 16 + p)
        )

    def mine(b):
        return (b // 2 == t) & (t == z)

    def hand_on(b):
        g_wait(b, 0)
        g_fwd(b).start()

    def step1(b):
        rows = pl.ds(mult(b * BLK, BLK), BLK)
        g_wait(b, 1)
        g_wait(b, 2)
        out = lax.dot_general(
            headv[...], gs[rows, :], (((1,), (1,)), ((), ())), preferred_element_type=F32
        )
        for i in range(4):
            for j in range(4):
                first = ROWS * (4 * i + j)
                pb[b, i + h * (j - i), j + h * (i - j)] = out[first : first + ROWS]
        for i in range(2):
            for cp in copies_a(b, i):
                cp.start()

    def pass_on(b):
        for i in range(2):
            k = 1 + 2 * i
            to_a, to_b = lax.rem(ca + k, 4), lax.rem(cb + k, 4)
            arrived(ax.at[b, i], ax_r.at[b, i])
            pb[b, 2 * i : 2 * i + 2, to_a, 0:32] += ax[b, i]
            arrived(ay.at[b, i], ay_r.at[b, i])
            pb[b, to_b, 2 * i : 2 * i + 2, 32:56] += ay[b, i]
            for cp in copies_b(b, i):
                cp.start()

    def step2(b):
        for i in range(2):
            arrived(r1x.at[b, i], r1x_r.at[b, i])
            arrived(r1y.at[b, i], r1y_r.at[b, i])
        s1x[b] = pb[b, :, ca, 0:32] + r1x[b, 0] + r1x[b, 1]
        s1y[b] = pb[b, cb, :, 32:56] + r1y[b, 0] + r1y[b, 1]
        for k in (2, 1, 3):
            for cp in copies2(b, k):
                cp.start()

    def step3(b):
        for k in (1, 2, 3):
            arrived(r2x.at[b, k - 1], r2x_r.at[b, k - 1])
            arrived(r2y.at[b, k - 1], r2y_r.at[b, k - 1])
        s2[b, 0:32] = (s1x[b, cb] + r2x[b, 0]) + (r2x[b, 1] + r2x[b, 2])
        s2[b, 32:56] = (s1y[b, ca] + r2y[b, 0]) + (r2y[b, 1] + r2y[b, 2])

        @pl.when(mine(b))
        def _():
            fin[z, lax.rem(b, 2)] = s2[b]

        @pl.when(jnp.logical_not(mine(b)))
        def _():
            copy3(b).start()

    def group_term(g, i, half):
        term = jnp.dot(
            hid_t[128 * i : 128 * (i + 1), pl.ds(mult(g * TG, TG), TG)],
            gs[pl.ds(mult(g * TG, TG), TG), 1024 * half : 1024 * (half + 1)],
            preferred_element_type=F32,
        )
        return term.astype(BF16).astype(F32)

    def add_group(g, half):
        for i in range(7):
            rows = slice(128 * i, 128 * (i + 1))
            cols = slice(1024 * half, 1024 * (half + 1))
            new = acc[rows, cols] + group_term(g, i, half)
            acc[rows, cols] = new
            out = new.astype(BF16)
            for j in range(2):
                at = mult(COLS * order[2 * half + j], COLS)
                gh[rows, pl.ds(at, COLS)] = out[:, COLS * j : COLS * (j + 1)]

    hand_on(0)
    hand_on(1)

    def when(condition, step, *args):
        @pl.when(condition)
        def _():
            step(*args)

    def block(i, _):
        odd = lax.rem(i, 2) == 1
        when(i < 8, step1, i)
        when(i < 6, hand_on, i + 2)
        when((i > 0) & (i < 9), pass_on, i - 1)
        when(odd & (i < 8), add_group, i // 2, 0)
        when(jnp.logical_not(odd) & (i > 0) & (i < 9), add_group, i // 2 - 1, 1)
        when((i > 1) & (i < 10), step2, i - 2)
        when(i > 3, step3, i - 4)
        return 0

    lax.fori_loop(0, 12, block, 0)

    for s in range(2):
        for k in range(4):

            @pl.when(jnp.logical_not((t == z) & (z == k)))
            def _():
                arrived(fin.at[k, s], f_r.at[k, s])

        hg[:, 128 * s : 128 * (s + 1)] = (
            (fin[0, s] + fin[1, s]) + (fin[2, s] + fin[3, s])
        ).astype(BF16)

    for cp in (h_cross, h_pair, h_sib, fwd1, fwd2):
        cp.wait_send()

    def drain(k, _):
        spread_copy(k).wait_send()
        ta_copy(k).wait_send()
        tb_copy(k).wait_send()
        t1_copy(k).wait_send()
        t2_copy(k).wait_send()
        la_copy(k).wait_send()
        lb_copy(k).wait_send()
        lc_copy(k).wait_send()
        return 0

    lax.fori_loop(1, 16, drain, 0)

    def drain_blocks(b, _):
        g_cross(b).wait_send()
        g_sib(b).wait_send()
        g_fwd(b).wait_send()
        for i in range(2):
            for cp in copies_a(b, i) + copies_b(b, i):
                cp.wait_send()
        for k in (1, 2, 3):
            for cp in copies2(b, k):
                cp.wait_send()

        @pl.when(jnp.logical_not(mine(b)))
        def _():
            copy3(b).wait_send()

        return 0

    lax.fori_loop(0, NB, drain_blocks, 0)


def hand_over(hg_in, gh_in, hg, gh, sem):
    a = pltpu.make_async_copy(hg_in, hg, sem.at[0])
    b = pltpu.make_async_copy(gh_in, gh, sem.at[1])
    a.start()
    b.start()
    a.wait()
    b.wait()


def body(hidden_states, student_head, teacher_logits, quality):
    teach = (
        teacher_logits.reshape(4, 256, 4, 128).transpose(1, 2, 0, 3).reshape(4, 16, 4, 16, 128)
    )
    hbm = pl.BlockSpec(memory_space=pltpu.HBM)
    vmem = pl.BlockSpec(memory_space=pltpu.VMEM)
    dma = pltpu.SemaphoreType.DMA
    hg, gh = pl.pallas_call(
        kernel,
        name="distill_backward",
        out_shape=(pltpu.VMEM((ROWS, TG), BF16), pltpu.VMEM((DS, 2048), BF16)),
        in_specs=[hbm, hbm, hbm, vmem],
        out_specs=(vmem, vmem),
        scratch_shapes=[
            pltpu.VMEM((TOK, D), BF16),
            pltpu.VMEM((DS, 2048), BF16),
            pltpu.VMEM((4, DS, COLS), BF16),
            pltpu.VMEM((4, 16, 4, 16, 128), BF16),
            pltpu.VMEM((8, 2, 4, 4, 16, 128), BF16),
            pltpu.VMEM((16, 8, 2, 16, 128), BF16),
            pltpu.VMEM((TOK, COLS), F32),
            pltpu.VMEM((TOK, 2048), BF16),
            pltpu.VMEM((DS, TOK), BF16),
            pltpu.VMEM((DS, 2048), F32),
            pltpu.VMEM((NB, 4, 4, ROWS, BLK), F32),
            pltpu.VMEM((NB, 2, 2, 32, BLK), F32),
            pltpu.VMEM((NB, 2, 2, 24, BLK), F32),
            pltpu.VMEM((NB, 2, 4, 32, BLK), F32),
            pltpu.VMEM((NB, 2, 4, 24, BLK), F32),
            pltpu.VMEM((NB, 4, 32, BLK), F32),
            pltpu.VMEM((NB, 4, 24, BLK), F32),
            pltpu.VMEM((NB, 3, 32, BLK), F32),
            pltpu.VMEM((NB, 3, 24, BLK), F32),
            pltpu.VMEM((NB, ROWS, BLK), F32),
            pltpu.VMEM((4, 2, ROWS, BLK), F32),
            pltpu.VMEM((1, 128), F32),
            pltpu.VMEM((15, 1, 128), F32),
            pltpu.VMEM((16, 1, 128), F32),
            pltpu.VMEM((16, 1, 128), F32),
            pltpu.VMEM((15, 1, 128), F32),
            pltpu.VMEM((1, 128), F32),
            pltpu.VMEM((15, 1, 128), F32),
            pltpu.VMEM((16, 1, 128), F32),
            pltpu.VMEM((16, 1, 128), F32),
            dma((9,)),
            dma((4, 3)), dma((4, 4)),
            dma((5,)), dma((5,)),
            dma((15,)), dma((15,)),
            dma((15,)), dma((15,)),
            dma((16,)), dma((16,)),
            dma((15,)), dma((15,)),
            dma((15,)), dma((15,)),
            dma((15,)), dma((15,)),
            dma((15,)), dma((15,)),
            dma((15,)), dma((15,)),
            dma((NB, 3)), dma((NB, 3)),
            dma((NB, 2)), dma((NB, 2)),
            dma((NB, 2)), dma((NB, 2)),
            dma((NB, 2)), dma((NB, 2)),
            dma((NB, 2)), dma((NB, 2)),
            dma((NB, 3)), dma((NB, 3)),
            dma((NB, 3)), dma((NB, 3)),
            dma((NB,)), dma((4, 2)),
        ],
        compiler_params=pltpu.CompilerParams(
            collective_id=0, has_side_effects=True, vmem_limit_bytes=55 * 2**20
        ),
        cost_estimate=pl.CostEstimate(
            flops=3 * 2 * TOK * DS * 2048, bytes_accessed=15 * 2**20, transcendentals=2**21
        ),
    )(hidden_states, student_head, teach, quality.reshape(2, 128))
    hg, gh = pl.pallas_call(
        hand_over,
        name="results",
        out_shape=(
            jax.ShapeDtypeStruct((ROWS, TG), BF16),
            jax.ShapeDtypeStruct((DS, 2048), BF16),
        ),
        in_specs=[vmem, vmem],
        out_specs=(hbm, hbm),
        scratch_shapes=[dma((2,))],
        compiler_params=pltpu.CompilerParams(vmem_limit_bytes=2**20),
    )(
        pltpu.with_memory_space_constraint(hg, pltpu.VMEM),
        pltpu.with_memory_space_constraint(gh, pltpu.VMEM),
    )
    return hg.T, gh


def solution(mesh):
    return jax.shard_map(
        body,
        mesh=mesh,
        in_specs=(P("tok", None), P("tok", "voc"), P(("tok", "voc"), None), P("tok")),
        out_specs=(P("tok", "voc"), P("tok", "voc")),
        check_vma=False,
    )
```

time: 158 us -> 131 us (0.83)
  Pallas kernels: 152 us -> 130 us
  local copies, waits for them, and re-layouts: 5.73 us -> 0 us
    pallas_call x1 -> x2, Pallas kernels: 152 us -> 130 us  [the longest x1 128 us: body(): pl.pallas_call(kernel, name='distill_backward', out_shape=(pltpu.VMEM((RO...]
    unnamed x2 -> x0, local copies, waits for them, and re-layouts: 5.73 us -> none
where the time goes in v2:
time: 131 us; the launch traced here: 130 us
  Pallas kernels  130 us (99%)
    pallas_call x1, Pallas kernels, body(): pl.pallas_call(kernel, name='distill_backward', out_shape=(pltpu.VMEM((RO...  128 us

profile of v2, /device:TPU:33, one launch (start us, length us, event | category | flops | bytes accessed | tf_op | source)
XLA Modules:
  0.0 130.4 jit_solution(11325675960500642737)
XLA Ops:
  0.6 127.9 %distill_backward.1 = (bf16[56,256]{1,0:T(8,128)(2,1)S(1)}, bf16[896,2048]{1,0:T(8,128)(2,1)S(1)}) custom-call(bf16[256,3584]{1,0:T(8,128)(2,1)} %hid.1, bf16[896,2048]{1,0:T(8,128)(2,1)} %head.1, bf16[4,16,4,16,128]{4,3,2,1,0:T(8,128)(2,1)} %bitcast.7, f32[2,128]{1,0:T(2,128)} %bitcast.9), custom_call_target="tpu_custom_call" | custom-call | flops 11274289152 | bytes 15728640 | tf_op jit(solution)/shard_map/distill_backward/pallas_call | solution.py:647
  128.5 1.9 %results.1 = (bf16[56,256]{1,0:T(8,128)(2,1)}, bf16[896,2048]{1,0:T(8,128)(2,1)}) custom-call(bf16[56,256]{1,0:T(8,128)(2,1)S(1)} %get-tuple-element.6.hg_in, bf16[896,2048]{1,0:T(8,128)(2,1)S(1)} %get-tuple-element.7.gh_in), custom_call_target="tpu_custom_call" | custom-call | tf_op jit(solution)/shard_map/results/pallas_call | solution.py:711

commit v3 on v2

--- a/solution.py
+++ b/solution.py
@@ -17,6 +17,8 @@
 BLK = 128
 TB_SPLIT = 8
 NB = 8
+NX = 3
+NS = NB + NX
 ROWS = 56
 CHUNKS = ((0, 256), (256, 256), (512, 256), (768, 128))
 F32 = jnp.float32
@@ -29,12 +31,12 @@
 
 def kernel(
     hid, head, teach, qual, hg, gh,
-    hid_all, headv, hcols, tloc, ta, tb, stu, gs, hid_t, acc,
-    pb, ax, ay, r1x, r1y, s1x, s1y, r2x, r2y, s2, fin,
+    hid_all, headv, hcols, hxc, tloc, ta, tb, stu, gs, hid_t, acc,
+    pb, zx, zy, r1x, r1y, s1x, s1y, z2x, z2y, r2x, r2y, s2, fin,
     row_a, got_t, tq, st, got_a, row_b, got_b, full, scale,
-    loc, head_s, head_r, hid_s, hid_r, bc_s, bc_r, ta_s, ta_r, tb_s, tb_r,
+    loc, head_s, head_r, hx_s, hx_r, hid_s, hid_r, bc_s, bc_r, ta_s, ta_r, tb_s, tb_r,
     t1_s, t1_r, t2_s, t2_r, la_s, la_r, lb_s, lb_r, lc_s, lc_r, g_s, g_r,
-    ax_s, ax_r, ay_s, ay_r, r1x_s, r1x_r, r1y_s, r1y_r, r2x_s, r2x_r, r2y_s, r2y_r, f_s, f_r,
+    r1x_s, r1x_r, r1y_s, r1y_r, r2x_s, r2x_r, r2y_s, r2y_r, f_s, f_r,
 ):
     t = lax.axis_index("tok")
     v = lax.axis_index("voc")
@@ -97,9 +99,11 @@
 
     pr, pc = piece(0, p)
     mr, mc = piece(t, p)
-    h_cross = remote(hid.at[pr, pc], hid_all.at[mr, mc], hid_s.at[0], hid_r.at[0], (cross, v))
+    znb = lax.rem(z + 2 * c + 3, 4)
+    h_cross = remote(
+        hid.at[pr, pc], hid_all.at[mr, mc], hid_s.at[0], hid_r.at[0], (cross, znb * 16 + p)
+    )
     h_cross.start()
-    znb = lax.rem(z + 2 * c + 3, 4)
     h_pair = remote(
         hid.at[pl.ds(128, 128)], hid_all.at[pl.ds(mult(TG * t + 128, 128), 128)],
         hid_s.at[1], hid_r.at[1], (cross, znb * 16 + p),
@@ -281,24 +285,44 @@
         return 0
 
     lax.fori_loop(1, 16, wait_ta, 0)
+    def tb_copy(k):
+        q = lax.rem(tz + k, 16)
+        return remote(
+            ta.at[:, :, q % 4, q // 4], tb.at[tz], tb_s.at[k], tb_r.at[tz], tz_peer(k)
+        )
+
+    def is_early(k):
+        q = lax.rem(tz + k, 16)
+        t2, zq = q // 4, q % 4
+        return ((t2 // 2 != c) & (zq == znb)) | ((t2 == sib) & (zq == z))
+
+    def start_tb(k, _):
+        @pl.when(jnp.logical_not(is_early(k)))
+        def _():
+            tb_copy(k).start()
+
+        return 0
+
+    def start_early(k, _):
+        @pl.when(is_early(k))
+        def _():
+            tb_copy(k).start()
+
+        return 0
+
+    lax.fori_loop(1, 16, start_early, 0)
     wait_head(cross, 3)
     wait_head(diag, 3)
     for cp in heads:
         cp.wait_send()
-
-    def tb_copy(k):
-        q = lax.rem(tz + k, 16)
-        return remote(
-            ta.at[:, :, q % 4, q // 4], tb.at[tz], tb_s.at[k], tb_r.at[tz], tz_peer(k)
-        )
-
-    def start_tb(k, _):
-        tb_copy(k).start()
-        return 0
-
     lax.fori_loop(1, TB_SPLIT, start_tb, 0)
     c_tb = pltpu.make_async_copy(ta.at[:, :, z, t], tb.at[tz], tb_r.at[tz])
     c_tb.start()
+
+    c_hx = pltpu.make_async_copy(hcols.at[cross], hxc.at[:, pl.ds(0, COLS)], loc.at[9])
+    c_hx.start()
+    h_hx = remote(hcols.at[diag], hxc.at[:, pl.ds(COLS, COLS)], hx_s.at[0], hx_r.at[0], (sib, v))
+    h_hx.start()
 
     r0, rn = CHUNKS[3]
     multiply(cross, r0, rn, False)
@@ -424,11 +448,19 @@
             e = stu[rows, 128 * q : 128 * (q + 1)]
             g = e * sc - jnp.exp(teacher - tl)
             gs[rows, 128 * q : 128 * (q + 1)] = g.astype(BF16)
+        g_sib(b).start()
+
+        @pl.when(b < NB - NX)
+        def _():
+            g_cross(b).start()
+
+        return 0
+
+    lax.fori_loop(0, NB, make_grads, 0)
+    for b in range(NB - NX, NB):
         g_cross(b).start()
-        g_sib(b).start()
-        return 0
-
-    lax.fori_loop(0, NB, make_grads, 0)
+    c_hx.wait()
+    arrived(hxc.at[:, pl.ds(COLS, COLS)], hx_r.at[0])
     for cp in c_heads:
         cp.wait()
 
@@ -441,88 +473,89 @@
     def line_b(k):
         return (t, z * 16 + h * (y * 4 + lax.rem(x + k, 4)) + (1 - h) * (lax.rem(y + k, 4) * 4 + x))
 
-    def copies_a(b, i):
-        k = 1 + 2 * i
+    def copies1(b, k):
+        i = k - 1
         return (
-            remote(
-                pb.at[b, pl.ds(2 * i, 2), lax.rem(ca + 2, 4), pl.ds(0, 32)], ax.at[b, i],
-                ax_s.at[b, i], ax_r.at[b, i], line_a(k),
-            ),
-            remote(
-                pb.at[b, lax.rem(cb + 2, 4), pl.ds(2 * i, 2), pl.ds(32, 24)], ay.at[b, i],
-                ay_s.at[b, i], ay_r.at[b, i], line_b(k),
-            ),
-        )
-
-    def copies_b(b, i):
-        k = 1 + 2 * i
-        return (
-            remote(
-                pb.at[b, :, lax.rem(ca + k, 4), pl.ds(0, 32)], r1x.at[b, i],
-                r1x_s.at[b, i], r1x_r.at[b, i], line_a(k),
-            ),
-            remote(
-                pb.at[b, lax.rem(cb + k, 4), :, pl.ds(32, 24)], r1y.at[b, i],
-                r1y_s.at[b, i], r1y_r.at[b, i], line_b(k),
-            ),
+            remote(zx.at[b, i], r1x.at[b, i], r1x_s.at[b, i], r1x_r.at[b, i], line_a(k)),
+            remote(zy.at[b, i], r1y.at[b, i], r1y_s.at[b, i], r1y_r.at[b, i], line_b(k)),
         )
 
     def copies2(b, k):
         i = k - 1
         return (
-            remote(
-                s1x.at[b, lax.rem(cb + k, 4)], r2x.at[b, i], r2x_s.at[b, i], r2x_r.at[b, i], line_b(k)
-            ),
-            remote(
-                s1y.at[b, lax.rem(ca + k, 4)], r2y.at[b, i], r2y_s.at[b, i], r2y_r.at[b, i], line_a(k)
-            ),
-        )
-
-    def copy3(b):
-        return remote(
-            s2.at[b], fin.at[z, lax.rem(b, 2)], f_s.at[b], f_r.at[z, lax.rem(b, 2)], (b // 2, t * 16 + p)
-        )
-
-    def mine(b):
-        return (b // 2 == t) & (t == z)
+            remote(z2x.at[b, i], r2x.at[b, i], r2x_s.at[b, i], r2x_r.at[b, i], line_b(k)),
+            remote(z2y.at[b, i], r2y.at[b, i], r2y_s.at[b, i], r2y_r.at[b, i], line_a(k)),
+        )
+
+    def block_of(n):
+        return n - NX * (n // NB)
+
+    def run_of(n):
+        return t + (n // NB) * (cross - t)
+
+    def copy3(n):
+        b = block_of(n)
+        at = (n // NB, z, lax.rem(b, 2))
+        return remote(s2.at[n], fin.at[at], f_s.at[n], f_r.at[at], (b // 2, run_of(n) * 16 + p))
+
+    def mine(n):
+        return (block_of(n) // 2 == t) & (run_of(n) == z)
 
     def hand_on(b):
         g_wait(b, 0)
         g_fwd(b).start()
+
+    def dot_t(a, b):
+        return lax.dot_general(a, b, (((1,), (1,)), ((), ())), preferred_element_type=F32)
 
     def step1(b):
         rows = pl.ds(mult(b * BLK, BLK), BLK)
         g_wait(b, 1)
         g_wait(b, 2)
-        out = lax.dot_general(
-            headv[...], gs[rows, :], (((1,), (1,)), ((), ())), preferred_element_type=F32
-        )
-        for i in range(4):
+        keep(b, dot_t(headv[...], gs[rows, :]), 0)
+        spread(b)
+
+    def alone_blocks():
+        for b in range(NB - NX, NB):
+            g_wait(b, 1)
+        for n, rows_of in ((NB - NX, headv), (NB, hxc)):
+            for m in range(2):
+                out = dot_t(
+                    rows_of[448 * m : 448 * (m + 1), 0 : 2 * COLS],
+                    gs[BLK * (NB - NX) :, 0 : 2 * COLS],
+                )
+                for k in range(NX):
+                    keep(n + k, out[:, BLK * k : BLK * (k + 1)], 2 * m)
+        for k in range(NX):
+            spread(NB - NX + k)
+            spread(NB + k)
+
+    def keep(n, out, begin):
+        for i in range(begin, begin + out.shape[0] // (4 * ROWS)):
             for j in range(4):
-                first = ROWS * (4 * i + j)
-                pb[b, i + h * (j - i), j + h * (i - j)] = out[first : first + ROWS]
-        for i in range(2):
-            for cp in copies_a(b, i):
+                first = ROWS * (4 * (i - begin) + j)
+                pb[n, i + h * (j - i), j + h * (i - j)] = out[first : first + ROWS]
+
+    def spread(b):
+        for k in (2, 1, 3):
+            to_a, to_b = lax.rem(ca + k, 4), lax.rem(cb + k, 4)
+            zx[b, k - 1] = pb[b, :, to_a, 0:32].reshape(128, BLK).astype(BF16)
+            zy[b, k - 1] = pb[b, to_b, :, 32:56].reshape(96, BLK).astype(BF16)
+            for cp in copies1(b, k):
                 cp.start()
 
-    def pass_on(b):
-        for i in range(2):
-            k = 1 + 2 * i
-            to_a, to_b = lax.rem(ca + k, 4), lax.rem(cb + k, 4)
-            arrived(ax.at[b, i], ax_r.at[b, i])
-            pb[b, 2 * i : 2 * i + 2, to_a, 0:32] += ax[b, i]
-            arrived(ay.at[b, i], ay_r.at[b, i])
-            pb[b, to_b, 2 * i : 2 * i + 2, 32:56] += ay[b, i]
-            for cp in copies_b(b, i):
-                cp.start()
-
     def step2(b):
-        for i in range(2):
+        for i in range(3):
             arrived(r1x.at[b, i], r1x_r.at[b, i])
             arrived(r1y.at[b, i], r1y_r.at[b, i])
-        s1x[b] = pb[b, :, ca, 0:32] + r1x[b, 0] + r1x[b, 1]
-        s1y[b] = pb[b, cb, :, 32:56] + r1y[b, 0] + r1y[b, 1]
+        from_a = (r1x[b, 0].astype(F32) + r1x[b, 1].astype(F32)) + r1x[b, 2].astype(F32)
+        from_b = (r1y[b, 0].astype(F32) + r1y[b, 1].astype(F32)) + r1y[b, 2].astype(F32)
+        s1x[b] = pb[b, :, ca, 0:32] + from_a.reshape(4, 32, BLK)
+        s1y[b] = pb[b, cb, :, 32:56] + from_b.reshape(4, 24, BLK)
         for k in (2, 1, 3):
+            z2x[b, k - 1] = s1x[b, lax.rem(cb + k, 4)].astype(BF16)
+            tail = jnp.zeros((8, BLK), F32)
+            z2y[b, k - 1] = jnp.concatenate([s1y[b, lax.rem(ca + k, 4)], tail], axis=0).astype(BF16)
             for cp in copies2(b, k):
                 cp.start()
 
@@ -530,12 +563,14 @@
         for k in (1, 2, 3):
             arrived(r2x.at[b, k - 1], r2x_r.at[b, k - 1])
             arrived(r2y.at[b, k - 1], r2y_r.at[b, k - 1])
-        s2[b, 0:32] = (s1x[b, cb] + r2x[b, 0]) + (r2x[b, 1] + r2x[b, 2])
-        s2[b, 32:56] = (s1y[b, ca] + r2y[b, 0]) + (r2y[b, 1] + r2y[b, 2])
+        from_b = (r2x[b, 0].astype(F32) + r2x[b, 1].astype(F32)) + r2x[b, 2].astype(F32)
+        from_a = (r2y[b, 0].astype(F32) + r2y[b, 1].astype(F32)) + r2y[b, 2].astype(F32)
+        s2[b, 0:32] = s1x[b, cb] + from_b
+        s2[b, 32:56] = s1y[b, ca] + from_a[0:24]
 
         @pl.when(mine(b))
         def _():
-            fin[z, lax.rem(b, 2)] = s2[b]
+            fin[b // NB, z, lax.rem(block_of(b), 2)] = s2[b]
 
         @pl.when(jnp.logical_not(mine(b)))
         def _():
@@ -560,39 +595,77 @@
                 at = mult(COLS * order[2 * half + j], COLS)
                 gh[rows, pl.ds(at, COLS)] = out[:, COLS * j : COLS * (j + 1)]
 
-    hand_on(0)
-    hand_on(1)
-
     def when(condition, step, *args):
         @pl.when(condition)
         def _():
             step(*args)
 
+    alone_blocks()
+    hand_on(0)
+
+    def early2(i):
+        step2(NB - NX + i)
+        step2(NB + i)
+
+    def early3(i):
+        step3(NB - NX + i)
+        step3(NB + i)
+
+    def late_waits():
+        g_wait(6, 2)
+        g_wait(7, 2)
+
     def block(i, _):
-        odd = lax.rem(i, 2) == 1
-        when(i < 8, step1, i)
-        when(i < 6, hand_on, i + 2)
-        when((i > 0) & (i < 9), pass_on, i - 1)
-        when(odd & (i < 8), add_group, i // 2, 0)
-        when(jnp.logical_not(odd) & (i > 0) & (i < 9), add_group, i // 2 - 1, 1)
-        when((i > 1) & (i < 10), step2, i - 2)
-        when(i > 3, step3, i - 4)
-        return 0
-
-    lax.fori_loop(0, 12, block, 0)
-
-    for s in range(2):
+        when(i < 5, step1, i)
+        when(i < 4, hand_on, i + 1)
+        when((i > 1) & (i < 5), early2, i - 2)
+        when((i > 2) & (i < 8), step2, i - 3)
+        when(i == 5, hand_on, 5)
+        when(i == 6, g_wait, 5, 2)
+        when(i == 8, step3, 3)
+        when(i == 8, step3, 4)
+        when(i == 8, hand_on, 7)
+        when(i == 8, late_waits)
+        g = (i - 1 - i // 5) // 2
+        first = (i == 1) | (i == 3) | (i == 6) | (i == 8)
+        when(first, add_group, g, 0)
+        when((i > 0) & (i != 5) & jnp.logical_not(first), add_group, g, 1)
+        when((i > 4) & (i < 8), early3, i - 5)
+        when(i == 6, step3, 0)
+        when(i == 7, step3, 1)
+        when(i == 7, step3, 2)
+        when(i == 7, hand_on, 6)
+        return 0
+
+    lax.fori_loop(0, 10, block, 0)
+
+    for half in range(2):
+        cols = slice(128 * half, 128 * (half + 1))
         for k in range(4):
 
             @pl.when(jnp.logical_not((t == z) & (z == k)))
             def _():
-                arrived(fin.at[k, s], f_r.at[k, s])
-
-        hg[:, 128 * s : 128 * (s + 1)] = (
-            (fin[0, s] + fin[1, s]) + (fin[2, s] + fin[3, s])
-        ).astype(BF16)
-
-    for cp in (h_cross, h_pair, h_sib, fwd1, fwd2):
+                arrived(fin.at[0, k, half], f_r.at[0, k, half])
+
+        near = (fin[0, 0, half] + fin[0, 1, half]) + (fin[0, 2, half] + fin[0, 3, half])
+        alone = 2 * t + half >= NB - NX
+
+        @pl.when(jnp.logical_not(alone))
+        def _():
+            hg[:, cols] = near.astype(BF16)
+
+        @pl.when(alone)
+        def _():
+            for k in range(4):
+
+                @pl.when(jnp.logical_not((lax.rem(t + 2, 4) == z) & (z == k)))
+                def _():
+                    arrived(fin.at[1, k, half], f_r.at[1, k, half])
+
+            rest = (fin[1, 0, half] + fin[1, 1, half]) + (fin[1, 2, half] + fin[1, 3, half])
+            hg[:, cols] = (near + rest).astype(BF16)
+
+    for cp in (h_cross, h_pair, h_sib, fwd1, fwd2, h_hx):
         cp.wait_send()
 
     def drain(k, _):
@@ -612,19 +685,20 @@
         g_cross(b).wait_send()
         g_sib(b).wait_send()
         g_fwd(b).wait_send()
-        for i in range(2):
-            for cp in copies_a(b, i) + copies_b(b, i):
+        return 0
+
+    def drain_sums(n, _):
+        for k in (1, 2, 3):
+            for cp in copies1(n, k) + copies2(n, k):
                 cp.wait_send()
-        for k in (1, 2, 3):
-            for cp in copies2(b, k):
-                cp.wait_send()
-
-        @pl.when(jnp.logical_not(mine(b)))
+
+        @pl.when(jnp.logical_not(mine(n)))
         def _():
-            copy3(b).wait_send()
-
-        return 0
-
+            copy3(n).wait_send()
+
+        return 0
+
+    lax.fori_loop(0, NS, drain_sums, 0)
     lax.fori_loop(0, NB, drain_blocks, 0)
 
 
@@ -654,6 +728,7 @@
             pltpu.VMEM((TOK, D), BF16),
             pltpu.VMEM((DS, 2048), BF16),
             pltpu.VMEM((4, DS, COLS), BF16),
+            pltpu.VMEM((DS, 2 * COLS), BF16),
             pltpu.VMEM((4, 16, 4, 16, 128), BF16),
             pltpu.VMEM((8, 2, 4, 4, 16, 128), BF16),
             pltpu.VMEM((16, 8, 2, 16, 128), BF16),
@@ -661,17 +736,19 @@
             pltpu.VMEM((TOK, 2048), BF16),
             pltpu.VMEM((DS, TOK), BF16),
             pltpu.VMEM((DS, 2048), F32),
-            pltpu.VMEM((NB, 4, 4, ROWS, BLK), F32),
-            pltpu.VMEM((NB, 2, 2, 32, BLK), F32),
-            pltpu.VMEM((NB, 2, 2, 24, BLK), F32),
-            pltpu.VMEM((NB, 2, 4, 32, BLK), F32),
-            pltpu.VMEM((NB, 2, 4, 24, BLK), F32),
-            pltpu.VMEM((NB, 4, 32, BLK), F32),
-            pltpu.VMEM((NB, 4, 24, BLK), F32),
-            pltpu.VMEM((NB, 3, 32, BLK), F32),
-            pltpu.VMEM((NB, 3, 24, BLK), F32),
-            pltpu.VMEM((NB, ROWS, BLK), F32),
-            pltpu.VMEM((4, 2, ROWS, BLK), F32),
+            pltpu.VMEM((NS, 4, 4, ROWS, BLK), F32),
+            pltpu.VMEM((NS, 3, 128, BLK), BF16),
+            pltpu.VMEM((NS, 3, 96, BLK), BF16),
+            pltpu.VMEM((NS, 3, 128, BLK), BF16),
+            pltpu.VMEM((NS, 3, 96, BLK), BF16),
+            pltpu.VMEM((NS, 4, 32, BLK), F32),
+            pltpu.VMEM((NS, 4, 24, BLK), F32),
+            pltpu.VMEM((NS, 3, 32, BLK), BF16),
+            pltpu.VMEM((NS, 3, 32, BLK), BF16),
+            pltpu.VMEM((NS, 3, 32, BLK), BF16),
+            pltpu.VMEM((NS, 3, 32, BLK), BF16),
+            pltpu.VMEM((NS, ROWS, BLK), F32),
+            pltpu.VMEM((2, 4, 2, ROWS, BLK), F32),
             pltpu.VMEM((1, 128), F32),
             pltpu.VMEM((15, 1, 128), F32),
             pltpu.VMEM((16, 1, 128), F32),
@@ -681,8 +758,9 @@
             pltpu.VMEM((15, 1, 128), F32),
             pltpu.VMEM((16, 1, 128), F32),
             pltpu.VMEM((16, 1, 128), F32),
-            dma((9,)),
+            dma((10,)),
             dma((4, 3)), dma((4, 4)),
+            dma((1,)), dma((1,)),
             dma((5,)), dma((5,)),
             dma((15,)), dma((15,)),
             dma((15,)), dma((15,)),
@@ -693,13 +771,11 @@
             dma((15,)), dma((15,)),
             dma((15,)), dma((15,)),
             dma((NB, 3)), dma((NB, 3)),
-            dma((NB, 2)), dma((NB, 2)),
-            dma((NB, 2)), dma((NB, 2)),
-            dma((NB, 2)), dma((NB, 2)),
-            dma((NB, 2)), dma((NB, 2)),
-            dma((NB, 3)), dma((NB, 3)),
-            dma((NB, 3)), dma((NB, 3)),
-            dma((NB,)), dma((4, 2)),
+            dma((NS, 3)), dma((NS, 3)),
+            dma((NS, 3)), dma((NS, 3)),
+            dma((NS, 3)), dma((NS, 3)),
+            dma((NS, 3)), dma((NS, 3)),
+            dma((NS,)), dma((2, 4, 2)),
         ],
         compiler_params=pltpu.CompilerParams(
             collective_id=0, has_side_effects=True, vmem_limit_bytes=55 * 2**20

time: 131 us -> 118 us (0.901)
  the two profiles are of different devices: /device:TPU:33 before, /device:TPU:1 now
where the time goes in v3:
time: 118 us
  Pallas kernels  118 us (100%)
    pallas_call x1, Pallas kernels, body(): pl.pallas_call(kernel, name='distill_backward', out_shape=(pltpu.VMEM((RO...  116 us

profile of v3, /device:TPU:1, one launch (start us, length us, event | category | flops | bytes accessed | tf_op | source)
XLA Modules:
  0.0 118.4 jit_solution(2110057955618177273)
XLA Ops:
  0.6 115.9 %distill_backward.1 = (bf16[56,256]{1,0:T(8,128)(2,1)S(1)}, bf16[896,2048]{1,0:T(8,128)(2,1)S(1)}) custom-call(bf16[256,3584]{1,0:T(8,128)(2,1)} %hid.1, bf16[896,2048]{1,0:T(8,128)(2,1)} %head.1, bf16[4,16,4,16,128]{4,3,2,1,0:T(8,128)(2,1)} %bitcast.7, f32[2,128]{1,0:T(2,128)} %bitcast.9), custom_call_target="tpu_custom_call" | custom-call | flops 11274289152 | bytes 15728640 | tf_op jit(solution)/shard_map/distill_backward/pallas_call | solution.py:721
  116.5 1.9 %results.1 = (bf16[56,256]{1,0:T(8,128)(2,1)}, bf16[896,2048]{1,0:T(8,128)(2,1)}) custom-call(bf16[56,256]{1,0:T(8,128)(2,1)S(1)} %get-tuple-element.6.hg_in, bf16[896,2048]{1,0:T(8,128)(2,1)S(1)} %get-tuple-element.7.gh_in), custom_call_target="tpu_custom_call" | custom-call | tf_op jit(solution)/shard_map/results/pallas_call | solution.py:787

commit v4 on v3

--- a/solution.py
+++ b/solution.py
@@ -30,10 +30,10 @@
 
 
 def kernel(
-    hid, head, teach, qual, hg, gh,
+    hid, head, teach, qual_hbm, hg, gh,
     hid_all, headv, hcols, hxc, tloc, ta, tb, stu, gs, hid_t, acc,
     pb, zx, zy, r1x, r1y, s1x, s1y, z2x, z2y, r2x, r2y, s2, fin,
-    row_a, got_t, tq, st, got_a, row_b, got_b, full, scale,
+    qual, row_a, got_t, tq, st, got_a, row_b, got_b, full, scale,
     loc, head_s, head_r, hx_s, hx_r, hid_s, hid_r, bc_s, bc_r, ta_s, ta_r, tb_s, tb_r,
     t1_s, t1_r, t2_s, t2_r, la_s, la_r, lb_s, lb_r, lc_s, lc_r, g_s, g_r,
     r1x_s, r1x_r, r1y_s, r1y_r, r2x_s, r2x_r, r2y_s, r2y_r, f_s, f_r,
@@ -86,7 +86,8 @@
     ]
     c_tl = pltpu.make_async_copy(teach, tloc, loc.at[3])
     c_ta = pltpu.make_async_copy(teach.at[:, p], ta.at[p // 2, p % 2], loc.at[4])
-    for cp in (c_hid, c_own, c_tl, c_ta, *c_heads):
+    c_q = pltpu.make_async_copy(qual_hbm, qual, loc.at[10])
+    for cp in (c_hid, c_own, c_tl, c_ta, c_q, *c_heads):
         cp.start()
 
     pl.semaphore_wait(bar, 30)
@@ -212,6 +213,7 @@
 
     lax.fori_loop(1, 16, wait_t1, 0)
     tl_row = row_a[...] + jnp.sum(got_t[...], axis=0)
+    c_q.wait()
     q_row = qual[pl.ds(z // 2, 1), :]
     weight = LOSS_SCALE * jnp.where(lax.rem(z, 2) == 0, q_row, swap(q_row))
     tq[tz] = jnp.where(low, tl_row - jnp.log(weight), swap(weight))
@@ -341,7 +343,7 @@
         st[2 * b + 1] = jnp.where(low, swap(m_row), s_row)
         return 0
 
-    lax.fori_loop(0, NB, stats, 0)
+    lax.fori_loop(0, NB, stats, 0, unroll=4)
 
     def la_copy(k):
         return remote(
@@ -639,32 +641,6 @@
 
     lax.fori_loop(0, 10, block, 0)
 
-    for half in range(2):
-        cols = slice(128 * half, 128 * (half + 1))
-        for k in range(4):
-
-            @pl.when(jnp.logical_not((t == z) & (z == k)))
-            def _():
-                arrived(fin.at[0, k, half], f_r.at[0, k, half])
-
-        near = (fin[0, 0, half] + fin[0, 1, half]) + (fin[0, 2, half] + fin[0, 3, half])
-        alone = 2 * t + half >= NB - NX
-
-        @pl.when(jnp.logical_not(alone))
-        def _():
-            hg[:, cols] = near.astype(BF16)
-
-        @pl.when(alone)
-        def _():
-            for k in range(4):
-
-                @pl.when(jnp.logical_not((lax.rem(t + 2, 4) == z) & (z == k)))
-                def _():
-                    arrived(fin.at[1, k, half], f_r.at[1, k, half])
-
-            rest = (fin[1, 0, half] + fin[1, 1, half]) + (fin[1, 2, half] + fin[1, 3, half])
-            hg[:, cols] = (near + rest).astype(BF16)
-
     for cp in (h_cross, h_pair, h_sib, fwd1, fwd2, h_hx):
         cp.wait_send()
 
@@ -701,14 +677,42 @@
     lax.fori_loop(0, NS, drain_sums, 0)
     lax.fori_loop(0, NB, drain_blocks, 0)
 
+    for half in range(2):
+        cols = slice(128 * half, 128 * (half + 1))
+        for k in range(4):
+
+            @pl.when(jnp.logical_not((t == z) & (z == k)))
+            def _():
+                arrived(fin.at[0, k, half], f_r.at[0, k, half])
+
+        near = (fin[0, 0, half] + fin[0, 1, half]) + (fin[0, 2, half] + fin[0, 3, half])
+        alone = 2 * t + half >= NB - NX
+
+        @pl.when(jnp.logical_not(alone))
+        def _():
+            hg[:, cols] = near.astype(BF16)
+
+        @pl.when(alone)
+        def _():
+            for k in range(4):
+
+                @pl.when(jnp.logical_not((lax.rem(t + 2, 4) == z) & (z == k)))
+                def _():
+                    arrived(fin.at[1, k, half], f_r.at[1, k, half])
+
+            rest = (fin[1, 0, half] + fin[1, 1, half]) + (fin[1, 2, half] + fin[1, 3, half])
+            hg[:, cols] = (near + rest).astype(BF16)
+
 
 def hand_over(hg_in, gh_in, hg, gh, sem):
-    a = pltpu.make_async_copy(hg_in, hg, sem.at[0])
-    b = pltpu.make_async_copy(gh_in, gh, sem.at[1])
-    a.start()
-    b.start()
-    a.wait()
-    b.wait()
+    copies = [pltpu.make_async_copy(hg_in, hg, sem.at[7])]
+    for i in range(7):
+        rows = pl.ds(128 * i, 128)
+        copies.append(pltpu.make_async_copy(gh_in.at[rows], gh.at[rows], sem.at[i]))
+    for cp in copies:
+        cp.start()
+    for cp in copies:
+        cp.wait()
 
 
 def body(hidden_states, student_head, teacher_logits, quality):
@@ -722,7 +726,7 @@
         kernel,
         name="distill_backward",
         out_shape=(pltpu.VMEM((ROWS, TG), BF16), pltpu.VMEM((DS, 2048), BF16)),
-        in_specs=[hbm, hbm, hbm, vmem],
+        in_specs=[hbm, hbm, hbm, hbm],
         out_specs=(vmem, vmem),
         scratch_shapes=[
             pltpu.VMEM((TOK, D), BF16),
@@ -749,6 +753,7 @@
             pltpu.VMEM((NS, 3, 32, BLK), BF16),
             pltpu.VMEM((NS, ROWS, BLK), F32),
             pltpu.VMEM((2, 4, 2, ROWS, BLK), F32),
+            pltpu.VMEM((2, 128), F32),
             pltpu.VMEM((1, 128), F32),
             pltpu.VMEM((15, 1, 128), F32),
             pltpu.VMEM((16, 1, 128), F32),
@@ -758,7 +763,7 @@
             pltpu.VMEM((15, 1, 128), F32),
             pltpu.VMEM((16, 1, 128), F32),
             pltpu.VMEM((16, 1, 128), F32),
-            dma((10,)),
+            dma((11,)),
             dma((4, 3)), dma((4, 4)),
             dma((1,)), dma((1,)),
             dma((5,)), dma((5,)),
@@ -793,7 +798,7 @@
         ),
         in_specs=[vmem, vmem],
         out_specs=(hbm, hbm),
-        scratch_shapes=[dma((2,))],
+        scratch_shapes=[dma((8,))],
         compiler_params=pltpu.CompilerParams(vmem_limit_bytes=2**20),
     )(
         pltpu.with_memory_space_constraint(hg, pltpu.VMEM),

time: 118 us -> 117 us (level)
  Pallas kernels: 118 us -> 116 us
    pallas_call x1, Pallas kernels: 116 us -> 115 us  [body(): pl.pallas_call(kernel, name='distill_backward', out_shape=(pltpu.VMEM((RO...]
where the time goes in v4:
time: 117 us
  Pallas kernels  116 us (99%)
    pallas_call x1, Pallas kernels, body(): pl.pallas_call(kernel, name='distill_backward', out_shape=(pltpu.VMEM((RO...  115 us

profile of v4, /device:TPU:1, one launch (start us, length us, event | category | flops | bytes accessed | tf_op | source)
XLA Modules:
  0.0 117.1 jit_solution(8942942910052631631)
XLA Ops:
  0.6 114.5 %distill_backward.1 = (bf16[56,256]{1,0:T(8,128)(2,1)S(1)}, bf16[896,2048]{1,0:T(8,128)(2,1)S(1)}) custom-call(bf16[256,3584]{1,0:T(8,128)(2,1)} %hid.1, bf16[896,2048]{1,0:T(8,128)(2,1)} %head.1, bf16[4,16,4,16,128]{4,3,2,1,0:T(8,128)(2,1)} %bitcast.7, f32[2,128]{1,0:T(2,128)} %bitcast.9), custom_call_target="tpu_custom_call" | custom-call | flops 11274289152 | bytes 15728640 | tf_op jit(solution)/shard_map/distill_backward/pallas_call | solution.py:725
  115.2 1.9 %results.1 = (bf16[56,256]{1,0:T(8,128)(2,1)}, bf16[896,2048]{1,0:T(8,128)(2,1)}) custom-call(bf16[56,256]{1,0:T(8,128)(2,1)S(1)} %get-tuple-element.6.hg_in, bf16[896,2048]{1,0:T(8,128)(2,1)S(1)} %get-tuple-element.7.gh_in), custom_call_target="tpu_custom_call" | custom-call | tf_op jit(solution)/shard_map/results/pallas_call | solution.py:792

commit v5 on v4

--- a/solution.py
+++ b/solution.py
@@ -567,8 +567,9 @@
             arrived(r2y.at[b, k - 1], r2y_r.at[b, k - 1])
         from_b = (r2x[b, 0].astype(F32) + r2x[b, 1].astype(F32)) + r2x[b, 2].astype(F32)
         from_a = (r2y[b, 0].astype(F32) + r2y[b, 1].astype(F32)) + r2y[b, 2].astype(F32)
-        s2[b, 0:32] = s1x[b, cb] + from_b
-        s2[b, 32:56] = s1y[b, ca] + from_a[0:24]
+        s2[b, 0:32] = (s1x[b, cb] + from_b).astype(BF16)
+        pad = jnp.zeros((8, BLK), F32)
+        s2[b, 32:64] = jnp.concatenate([s1y[b, ca] + from_a[0:24], pad], axis=0).astype(BF16)
 
         @pl.when(mine(b))
         def _():
@@ -629,9 +630,9 @@
         when(i == 8, hand_on, 7)
         when(i == 8, late_waits)
         g = (i - 1 - i // 5) // 2
-        first = (i == 1) | (i == 3) | (i == 6) | (i == 8)
+        first = (i == 1) | (i == 4) | (i == 6) | (i == 8)
         when(first, add_group, g, 0)
-        when((i > 0) & (i != 5) & jnp.logical_not(first), add_group, g, 1)
+        when((i > 0) & (i != 3) & jnp.logical_not(first), add_group, g, 1)
         when((i > 4) & (i < 8), early3, i - 5)
         when(i == 6, step3, 0)
         when(i == 7, step3, 1)
@@ -679,13 +680,17 @@
 
     for half in range(2):
         cols = slice(128 * half, 128 * (half + 1))
+
+        def part(source, k, half=half):
+            return fin[source, k, half].astype(F32)[0:ROWS]
+
         for k in range(4):
 
             @pl.when(jnp.logical_not((t == z) & (z == k)))
             def _():
                 arrived(fin.at[0, k, half], f_r.at[0, k, half])
 
-        near = (fin[0, 0, half] + fin[0, 1, half]) + (fin[0, 2, half] + fin[0, 3, half])
+        near = (part(0, 0) + part(0, 1)) + (part(0, 2) + part(0, 3))
         alone = 2 * t + half >= NB - NX
 
         @pl.when(jnp.logical_not(alone))
@@ -700,7 +705,7 @@
                 def _():
                     arrived(fin.at[1, k, half], f_r.at[1, k, half])
 
-            rest = (fin[1, 0, half] + fin[1, 1, half]) + (fin[1, 2, half] + fin[1, 3, half])
+            rest = (part(1, 0) + part(1, 1)) + (part(1, 2) + part(1, 3))
             hg[:, cols] = (near + rest).astype(BF16)
 
 
@@ -751,8 +756,8 @@
             pltpu.VMEM((NS, 3, 32, BLK), BF16),
             pltpu.VMEM((NS, 3, 32, BLK), BF16),
             pltpu.VMEM((NS, 3, 32, BLK), BF16),
-            pltpu.VMEM((NS, ROWS, BLK), F32),
-            pltpu.VMEM((2, 4, 2, ROWS, BLK), F32),
+            pltpu.VMEM((NS, 64, BLK), BF16),
+            pltpu.VMEM((2, 4, 2, 64, BLK), BF16),
             pltpu.VMEM((2, 128), F32),
             pltpu.VMEM((1, 128), F32),
             pltpu.VMEM((15, 1, 128), F32),

time: 117 us -> 116 us (level)
  no operation moved by 1% of the time
where the time goes in v5:
time: 116 us
  Pallas kernels  115 us (99%)
    pallas_call x1, Pallas kernels, body(): pl.pallas_call(kernel, name='distill_backward', out_shape=(pltpu.VMEM((RO...  113 us

profile of v5, /device:TPU:1, one launch (start us, length us, event | category | flops | bytes accessed | tf_op | source)
XLA Modules:
  0.0 116.0 jit_solution(12187665326258316513)
XLA Ops:
  0.6 113.4 %distill_backward.1 = (bf16[56,256]{1,0:T(8,128)(2,1)S(1)}, bf16[896,2048]{1,0:T(8,128)(2,1)S(1)}) custom-call(bf16[256,3584]{1,0:T(8,128)(2,1)} %hid.1, bf16[896,2048]{1,0:T(8,128)(2,1)} %head.1, bf16[4,16,4,16,128]{4,3,2,1,0:T(8,128)(2,1)} %bitcast.7, f32[2,128]{1,0:T(2,128)} %bitcast.9), custom_call_target="tpu_custom_call" | custom-call | flops 11274289152 | bytes 15728640 | tf_op jit(solution)/shard_map/distill_backward/pallas_call | solution.py:730
  114.1 1.9 %results.1 = (bf16[56,256]{1,0:T(8,128)(2,1)}, bf16[896,2048]{1,0:T(8,128)(2,1)}) custom-call(bf16[56,256]{1,0:T(8,128)(2,1)S(1)} %get-tuple-element.6.hg_in, bf16[896,2048]{1,0:T(8,128)(2,1)S(1)} %get-tuple-element.7.gh_in), custom_call_target="tpu_custom_call" | custom-call | tf_op jit(solution)/shard_map/results/pallas_call | solution.py:797
